TPU v7x, 768 devices: a whole 4x8x12 slice. The times are simulated.
768 devices in a mesh: dp: 96 (over z, y), sub: 8 (over x, core).
Axes of the slice: x: 4, y: 8, z: 12, core: 2. Of those that a mesh axis runs over, the one named last changes fastest.
Arguments:
- embeddings: bfloat16 [393216, 1024], P(('dp', 'sub')), may hold values from -6 to 6
- rotation: bfloat16 [1024, 1024], replicated, may hold values from -0.1875 to 0.1875
- centroids: bfloat16 [96, 1024], replicated, may hold values from -6 to 6
- assignments: int32 [393216], P(('dp', 'sub')), may hold values from 0 to 95
- codes: int32 [393216, 64], P(('dp', 'sub')), may hold values from 0 to 255
Outputs:
- gram: float32 [1024, 1024], P('sub')
- coarse_sums: float32 [96, 1024], P('dp', 'sub')
- codebook_sums: float32 [256, 1024], P(None, 'sub')
All inputs are finite; a program needn't handle non-finite values.
Results may differ from a plain program's by a relative error of at most 0.0045.
Values may be sent and summed in bfloat16 or wider, within the bound.
No kernel may reach another device: no remote copies, remote signals or barrier semaphores. Data moves between devices by JAX's collectives and lax.ppermute only.
A program may use at most 32 MiB of HBM per device.

v0:
```python
import jax
import jax.numpy as jnp
from jax import lax
from jax.sharding import Mesh
from jax.sharding import PartitionSpec as P

D = 1024
M = 64
K = 256
DP = ("dp_0", "dp_1")
DP_SUB = ("dp_0", "dp_1", "sub")


def split_up(x, dim, peers):
    shape = x.shape
    blocks = x.reshape(*shape[:dim], peers, shape[dim] // peers, *shape[dim + 1 :])
    return jnp.moveaxis(blocks, dim, 0)


def sent_and_summed(x, axis, dim):
    blocks = split_up(x, dim, lax.axis_size(axis))
    arrived = lax.all_to_all(blocks, axis, split_axis=0, concat_axis=0, tiled=True)
    return arrived.astype(jnp.float32).sum(axis=0)


def sum_in_order(blocks, axes, turns):
    shape = [lax.axis_size(a) for a in axes]
    blocks = blocks.reshape(*shape, *blocks.shape[1:])
    blocks = blocks.transpose(*turns, *range(len(axes), blocks.ndim))
    blocks = blocks.reshape(-1, *blocks.shape[len(axes) :])
    for k in turns:
        blocks = lax.psum_scatter(blocks, axes[k], scatter_dimension=0, tiled=True)
    return blocks[0]


def summed_rows(x, axes, turns, dim):
    peers = lax.axis_size(axes)
    return sum_in_order(split_up(x, dim, peers), axes, turns)


def together(arrays, axis):
    ends = [0]
    for a in arrays:
        ends.append(ends[-1] + a.size)
    subtotal = lax.psum(jnp.concatenate([a.ravel() for a in arrays]), axis)
    return tuple((subtotal[b:e].reshape(a.shape) for a, b, e in zip(arrays, ends, ends[1:])))


def contract_rows(left, right):
    return lax.dot_general(
        left, right, (((0,), (0,)), ((), ())), preferred_element_type=jnp.float32
    )


def per_device(embeddings, rotation, centroids, assignments, codes):
    vec_rows, width = embeddings.shape
    cent_total = centroids.shape[0]
    sub_count = lax.axis_size("sub")
    dp_count = lax.axis_size(DP)
    total_rows = vec_rows * sub_count * dp_count
    columns = embeddings
    gram_part = sent_and_summed(contract_rows(columns, embeddings).astype(jnp.bfloat16), "sub", 0)
    rotated = jnp.dot(embeddings, rotation, preferred_element_type=jnp.float32)
    labels = lax.broadcasted_iota(jnp.int32, (1, cent_total), 1)
    select = (assignments[:, None] == labels).astype(jnp.bfloat16)
    base = jnp.dot(select, centroids, preferred_element_type=jnp.float32)
    residual = (rotated - base).astype(jnp.bfloat16)
    onehot = (assignments[:, None] == lax.iota(jnp.int32, cent_total)[None, :]).astype(jnp.bfloat16)
    everything = contract_rows(onehot, residual)
    columns = sent_and_summed(everything.astype(jnp.bfloat16), "sub", 1)
    coarse = summed_rows(columns, DP, (1, 0), 0)
    coarse_sums = coarse * (cent_total / total_rows) ** 0.5
    code_words = codes.astype(jnp.bfloat16)
    moved, moved_codes = (
        lax.all_to_all(residual, "sub", split_axis=1, concat_axis=0, tiled=True),
        lax.all_to_all(code_words, "sub", split_axis=1, concat_axis=0, tiled=True),
    )
    local_m = codes.shape[1] // sub_count
    subw = D // M
    owner_codes = moved_codes.astype(jnp.int32)
    gathered_rows = moved.shape[0]
    words = lax.broadcasted_iota(jnp.int32, (1, 1, K), 2)
    onehot = (owner_codes[:, :, None] == words).astype(jnp.bfloat16)
    pieces = moved.reshape(gathered_rows, local_m, subw)
    book_blocks = jnp.einsum("rmk,rms->kms", onehot, pieces, preferred_element_type=jnp.float32)
    book_local = book_blocks.reshape(K, local_m * subw)
    gram_sum, book_sum = together((gram_part, book_local), DP)
    gram = gram_sum / total_rows
    codebook_sums = book_sum * (K / total_rows) ** 0.5
    return (gram, coarse_sums, codebook_sums)


def solution(mesh):
    finer = Mesh(mesh.devices.reshape(12, 8, mesh.shape["sub"]), ("dp_0", "dp_1", "sub"))
    return jax.shard_map(
        per_device,
        mesh=finer,
        in_specs=(P(DP_SUB, None), P(), P(), P(DP_SUB), P(DP_SUB, None)),
        out_specs=(P("sub", None), P(DP, "sub"), P(None, "sub")),
        check_vma=False,
    )
```

profile of v0, /device:TPU:4, one launch (start us, length us, event | category | flops | bytes accessed | tf_op | source)
XLA Modules:
  0.0 318.1 jit_solution(16851833575297618620)
XLA Ops:
  7.2 0.0 copy-start
  7.2 1.7 convert_bitcast_fusion
  8.9 12.8 %all-to-all-start.2 = ((bf16[512,8,8]{0,2,1:T(8,128)(2,1)}), bf16[512,8,8]{0,2,1:T(8,128)(2,1)S(1)}, u32[]{:S(2)}, u32[]{:S(2)}) async-start(bf16[512,8,8]{0,2,1:T(8,128)(2,1)} %convert_bitcast_fusion), calls=%async_computation.2 | async-start | bytes 131072 | tf_op jit(solution)/shard_map/all_to_all | solution.py:76
  21.7 0.0 copy-done
  21.7 0.0 copy-start.1
  21.7 0.0 copy-start.2
  21.7 2.5 fusion.9
  24.2 0.0 copy-done.1
  24.2 0.0 copy-done.2
  24.2 0.5 subtract_convert_fusion
  24.7 1.2 copy_bitcast_fusion
  25.9 0.0 all-to-all-done.2
  25.9 5.5 %all-to-all-start.1 = ((bf16[512,8,128]{2,0,1:T(8,128)(2,1)}), bf16[512,8,128]{2,0,1:T(8,128)(2,1)}, u32[]{:S(2)}, u32[]{:S(2)}) async-start(bf16[512,8,128]{2,0,1:T(8,128)(2,1)} %copy_bitcast_fusion), calls=%async_computation.1 | async-start | bytes 2097152 | tf_op jit(solution)/shard_map/all_to_all | solution.py:75
  31.4 4.2 %convolution_convert_fusion = bf16[1024,1024]{1,0:T(8,128)(2,1)} fusion(bf16[512,1024]{1,0:T(8,128)(2,1)} %param.5), kind=kOutput, calls=%fused_computation.5 | convolution fusion | flops 1074790400 | bytes 3145728 | tf_op jit(solution)/shard_map/dot_general | solution.py:50
  35.6 8.7 %all-to-all-done.1 = bf16[512,8,128]{2,0,1:T(8,128)(2,1)} async-done(((bf16[512,8,128]{2,0,1:T(8,128)(2,1)}), bf16[512,8,128]{2,0,1:T(8,128)(2,1)}, u32[]{:S(2)}, u32[]{:S(2)}) %all-to-all-start.1) | async-done | bytes 1048608 | tf_op jit(solution)/shard_map/all_to_all | solution.py:75
  44.3 7.5 %all-to-all-start = ((bf16[8,128,1024]{2,1,0:T(8,128)(2,1)}), bf16[8,128,1024]{2,1,0:T(8,128)(2,1)}, u32[]{:S(2)}, u32[]{:S(2)}) async-start(bf16[8,128,1024]{2,1,0:T(8,128)(2,1)} %bitcast.44), calls=%async_computation | async-start | bytes 4194304 | tf_op jit(solution)/shard_map/all_to_all | solution.py:22
  51.8 0.0 all-reduce.4.cloned.1.call-start
  51.8 2.7 copy.15
  54.5 2.4 reshape.74
  56.9 7.7 %fusion.3 = f32[256,8,16]{0,2,1:T(8,128)S(1)} fusion(bf16[4096,8,16]{0,2,1:T(8,128)(2,1)} %reshape.74, s32[4096,8]{0,1:T(8,128)S(1)} %bitcast.48), kind=kOutput, calls=%fused_computation.8 | convolution fusion | flops 276824064 | bytes 1310720 | tf_op jit(solution)/shard_map/rmk,rms->kms/dot_general | solution.py:85
  64.5 1.3 copy.16
  65.9 1.5 reshape_reshape.6
  67.4 8.5 %all-to-all-done = bf16[8,128,1024]{2,1,0:T(8,128)(2,1)} async-done(((bf16[8,128,1024]{2,1,0:T(8,128)(2,1)}), bf16[8,128,1024]{2,1,0:T(8,128)(2,1)}, u32[]{:S(2)}, u32[]{:S(2)}) %all-to-all-start) | async-done | bytes 2097184 | tf_op jit(solution)/shard_map/all_to_all | solution.py:22
  75.9 2.0 convert_reduce_fusion
  77.9 0.1 copy.21
  78.0 0.9 pad_maximum_fusion
  78.9 0.0 all-reduce.4.cloned.1.call-update
  78.9 0.5 fusion.2
  79.4 0.7 copy.24
  80.1 6.5 %all-to-all-start.3 = ((bf16[8,96,128]{2,1,0:T(8,128)(2,1)}), bf16[8,96,128]{2,1,0:T(8,128)(2,1)S(1)}, u32[]{:S(2)}, u32[]{:S(2)}) async-start(bf16[8,96,128]{2,1,0:T(8,128)(2,1)} %bitcast.42), calls=%async_computation.3 | async-start | bytes 393216 | tf_op jit(solution)/shard_map/all_to_all | solution.py:22
  86.6 1.3 dynamic-slice.2
  87.9 1.3 dynamic-slice
  89.8 0.7 all-to-all-done.3
  90.6 0.1 copy.18
  90.6 27.4 %all-reduce = f32[96,1,128]{2,1,0:T(1,128)S(1)} all-reduce(f32[96,1,128]{2,1,0:T(1,128)S(1)} %bitcast.46), channel_id=2, replica_groups=mesh['dp_0'=12,'dp_1'=8,'sub'=8] {'dp_1'}, use_global_device_ids=true, to_apply=%region_3.0.clone | all-reduce | flops 12288 | bytes 98304
  118.1 29.0 %all-reduce.1 = f32[12,1,128]{2,1,0:T(1,128)S(1)} all-reduce(f32[12,1,128]{2,1,0:T(1,128)S(1)} %constant_dynamic-slice_fusion.1), channel_id=3, replica_groups=mesh['dp_0'=12,'dp_1'=8,'sub'=8] {'dp_0'}, use_global_device_ids=true, to_apply=%region_4.0.clone | all-reduce | flops 1536 | bytes 12288
  147.1 1.2 fusion.8
  148.3 159.4 %all-reduce.4.cloned.1.call-done = f32[163840]{0:T(1024)} async-done(((f32[163840]{0:T(1024)}), f32[163840]{0:T(1024)}) %all-reduce.4.cloned.1.call-update) | async-done | bytes 655376 | tf_op jit(solution)/shard_map/psum | solution.py:45
  307.7 1.1 slice_multiply_fusion
  308.8 0.9 div.10
  309.7 1.6 fusion.4
  (3 shorter events, 0.1 us)
Async XLA Ops:
  7.2 14.5 %copy-start = (bf16[1024,1024]{1,0:T(8,128)(2,1)S(1)}, bf16[1024,1024]{1,0:T(8,128)(2,1)}, u32[]{:S(2)}) copy-start(bf16[1024,1024]{1,0:T(8,128)(2,1)} %param.6) | copy-start | bytes 6291460
  8.9 17.0 %all-to-all-start.2 = ((bf16[512,8,8]{0,2,1:T(8,128)(2,1)}), bf16[512,8,8]{0,2,1:T(8,128)(2,1)S(1)}, u32[]{:S(2)}, u32[]{:S(2)}) async-start(bf16[512,8,8]{0,2,1:T(8,128)(2,1)} %convert_bitcast_fusion), calls=%async_computation.2 | async-start | bytes 131072 | tf_op jit(solution)/shard_map/all_to_all | solution.py:76
  21.7 2.5 copy-start.1
  21.7 2.5 copy-start.2
  25.9 18.4 %all-to-all-start.1 = ((bf16[512,8,128]{2,0,1:T(8,128)(2,1)}), bf16[512,8,128]{2,0,1:T(8,128)(2,1)}, u32[]{:S(2)}, u32[]{:S(2)}) async-start(bf16[512,8,128]{2,0,1:T(8,128)(2,1)} %copy_bitcast_fusion), calls=%async_computation.1 | async-start | bytes 2097152 | tf_op jit(solution)/shard_map/all_to_all | solution.py:75
  44.3 31.6 %all-to-all-start = ((bf16[8,128,1024]{2,1,0:T(8,128)(2,1)}), bf16[8,128,1024]{2,1,0:T(8,128)(2,1)}, u32[]{:S(2)}, u32[]{:S(2)}) async-start(bf16[8,128,1024]{2,1,0:T(8,128)(2,1)} %bitcast.44), calls=%async_computation | async-start | bytes 4194304 | tf_op jit(solution)/shard_map/all_to_all | solution.py:22
  51.8 255.9 %all-reduce.4.cloned.1.call-start = ((), (), s32[]{:S(2)}) async-start(), calls=%async_computation.4 | async-start | bytes 1310720 | tf_op jit(solution)/shard_map/psum | solution.py:45
  80.1 10.4 %all-to-all-start.3 = ((bf16[8,96,128]{2,1,0:T(8,128)(2,1)}), bf16[8,96,128]{2,1,0:T(8,128)(2,1)S(1)}, u32[]{:S(2)}, u32[]{:S(2)}) async-start(bf16[8,96,128]{2,1,0:T(8,128)(2,1)} %bitcast.42), calls=%async_computation.3 | async-start | bytes 393216 | tf_op jit(solution)/shard_map/all_to_all | solution.py:22
Sparse Core Ops, SparseCore 0:
  79.1 228.5 all-reduce.3
where the time goes:
time: 319 us; the launch traced here: 318 us
  waiting for transfers between devices  177 us (55%)
  blocking collectives  56.5 us (18%)
  starting transfers between devices  32.3 us (10%)
  matrix products  15.3 us (5%)
  between operations  14.8 us (5%)
  local copies, waits for them, and re-layouts  13.4 us (4%)
  other arithmetic  8.48 us (3%)
    psum x1, waiting for transfers between devices, together(): subtotal = lax.psum(jnp.concatenate([a.ravel() for a in arrays]), axis)  159 us
    unnamed x2, blocking collectives  56.5 us
    all_to_all x2, starting transfers between devices, sent_and_summed(): lax.all_to_all(blocks, axis, split_axis=0, concat_axis=0, tiled=True)  14 us
    all_to_all x1, starting transfers between devices, per_device(): lax.all_to_all(code_words, 'sub', split_axis=1, concat_axis=0, tiled=True)  12.8 us
    all_to_all x2, waiting for transfers between devices, sent_and_summed(): lax.all_to_all(blocks, axis, split_axis=0, concat_axis=0, tiled=True)  9.2 us
    all_to_all x1, waiting for transfers between devices, per_device(): lax.all_to_all(residual, 'sub', split_axis=1, concat_axis=0, tiled=True)  8.67 us
    dot_general x1, matrix products, per_device(): jnp.einsum('rmk,rms->kms', onehot, pieces, preferred_element_type=jnp.flo...  7.66 us
  transfers between devices with their start and end apart: 5, of which 4 were waited for; matrix products, arithmetic and copies ran while one was open for 9% of the time, Pallas kernels for 0%

commit v1 on v0

v1 whole, which is shorter than its diff:
```python
import jax
import jax.numpy as jnp
from jax import lax
from jax.experimental import pallas as pl
from jax.experimental.pallas import tpu as pltpu
from jax.sharding import Mesh
from jax.sharding import PartitionSpec as P

D = 1024
M = 64
K = 256
CENTS = 96
LANES = 128
X = 4
DP = ("z", "y")
DP_SUB = ("z", "y", "x", "c")
BOOK0 = D
COARSE0 = D + K
ROWS = D + K + CENTS
PIECE = 14
CHUNK = 16
bf16 = jnp.bfloat16
f16 = jnp.float16
f32 = jnp.float32
VMEM = pl.BlockSpec(memory_space=pltpu.VMEM)
SMEM = pl.BlockSpec(memory_space=pltpu.SMEM)


def dot(a, b):
    return jnp.dot(a, b, preferred_element_type=f32)


def partial_sums(core_ref, e0, e1, rot, cent, p0, p1, out, turned, res):
    core = core_ref[0]
    rows = e0.shape[0]
    halves = ((e0, p0), (e1, p1))

    def columns(x):
        return pl.ds(pl.multiple_of((2 * x + core) * LANES, LANES), LANES)

    for x in range(X):
        for h, (e, _) in enumerate(halves):
            turned[x * LANES : (x + 1) * LANES, h * rows : (h + 1) * rows] = e[:, columns(x)].T
    wide = 256
    for n in range(D // wide):
        cols = slice(n * wide, (n + 1) * wide)
        g = dot(turned[:, :rows], e0[:, cols]) + dot(turned[:, rows:], e1[:, cols])
        for x in range(X):
            for k in range(wide // LANES):
                j = n * (wide // LANES) + k
                out[x, j * LANES : (j + 1) * LANES, :] = g[
                    x * LANES : (x + 1) * LANES, k * LANES : (k + 1) * LANES
                ].astype(bf16)

    label = lax.broadcasted_iota(jnp.int32, (CENTS, rows), 0)
    picks = [(label == p[M : M + 1, :]).astype(bf16) for _, p in halves]
    for q in range(X // 2):
        r = jnp.concatenate([rot[:, columns(2 * q)], rot[:, columns(2 * q + 1)]], axis=1)
        c = jnp.concatenate([cent[:, columns(2 * q)], cent[:, columns(2 * q + 1)]], axis=1)
        coarse = jnp.zeros((CENTS, 2 * LANES), f32)
        for h, (e, _) in enumerate(halves):
            base = lax.dot_general(picks[h], c, (((0,), (0,)), ((), ())), preferred_element_type=f32)
            residual = (dot(e[...], r) - base).astype(bf16)
            res[h * rows : (h + 1) * rows, q * 2 * LANES : (q + 1) * 2 * LANES] = residual
            coarse += dot(picks[h], residual)
        for k in range(2):
            out[2 * q + k, COARSE0:ROWS, :] = coarse[:, k * LANES : (k + 1) * LANES].astype(bf16)

    word = lax.broadcasted_iota(jnp.int32, (K, rows), 0)
    lane = lax.broadcasted_iota(jnp.int32, (rows, LANES), 1)
    subs = M // 8

    def book(x, carry):
        total = jnp.zeros((K, LANES), f32)
        for h, (_, p) in enumerate(halves):
            first = pl.multiple_of((2 * x + core) * subs, subs)
            codes = p[pl.ds(first, subs), :]
            mine = res[h * rows : (h + 1) * rows, pl.ds(pl.multiple_of(x * LANES, LANES), LANES)]
            for m in range(subs):
                onehot = (word == codes[m : m + 1, :]).astype(bf16)
                part = jnp.where(lane // (LANES // subs) == m, mine, jnp.zeros_like(mine))
                total += dot(onehot, part)
        out[x, BOOK0:COARSE0, :] = total.astype(bf16)
        return carry

    lax.fori_loop(0, X, book, 0)


def first_sums(arrived, out, total):
    total[: ROWS, :] = arrived[...].astype(f32).sum(axis=0)
    peers = out.shape[0]
    zeros = jnp.zeros((CHUNK - PIECE - 1, LANES), f32)
    for i in range(peers):
        size = min(PIECE, max(0, COARSE0 - i * PIECE))
        parts = []
        if size:
            parts.append(total[i * PIECE : i * PIECE + size, :])
        if size < PIECE:
            parts.append(jnp.zeros((PIECE - size, LANES), f32))
        parts += [total[COARSE0 + i : COARSE0 + i + 1, :], zeros]
        out[i] = jnp.concatenate(parts, axis=0).astype(bf16)


def owned_sums(place_ref, arrived, coarse, mine, *, vectors):
    total = arrived[...].astype(f32).sum(axis=0)
    row = lax.broadcasted_iota(jnp.int32, (CHUNK, LANES), 0)
    coarse[...] = total[PIECE : PIECE + 1, :] * (CENTS / vectors) ** 0.5
    in_gram = place_ref[0] * PIECE + row < D
    total = total * jnp.where(in_gram, 1.0 / vectors, (K / vectors) ** 0.5)
    total = jnp.where(row < PIECE, total, 0.0)
    top = jnp.max(jnp.abs(total), keepdims=True)
    power = jnp.ceil(jnp.log2(jnp.maximum(top, 2.0**-100)))
    total = total * jnp.exp2(-power)
    total = jnp.where(row < PIECE, total, jnp.broadcast_to(power, total.shape))
    mine[...] = total


def laid_out(arrived, gram, book, flat):
    for i in range(arrived.shape[0]):
        size = min(PIECE, max(0, COARSE0 - i * PIECE))
        if size:
            piece = arrived[i]
            power = jnp.exp2(piece[PIECE : PIECE + 1, :])
            flat[i * PIECE : i * PIECE + size, :] = piece[:size] * power
    for j in range(D // LANES):
        gram[:, j * LANES : (j + 1) * LANES] = flat[j * LANES : (j + 1) * LANES, :]
    book[...] = flat[BOOK0:COARSE0, :]


def per_device(embeddings, rotation, centroids, assignments, codes):
    rows = embeddings.shape[0]
    peers = lax.axis_size(DP)
    vectors = rows * peers * lax.axis_size(("x", "c"))
    core = lax.axis_index("c").reshape(1)
    place = lax.axis_index(DP).reshape(1)
    words = jnp.concatenate([codes.T, jnp.broadcast_to(assignments[None, :], (8, rows))], axis=0)
    swap = [(0, 1), (1, 0)]
    other = lax.ppermute(embeddings, "c", swap)
    other_words = lax.ppermute(words, "c", swap)
    parts = pl.pallas_call(
        partial_sums,
        out_shape=jax.ShapeDtypeStruct((X, ROWS, LANES), bf16),
        in_specs=[SMEM] + [VMEM] * 6,
        out_specs=VMEM,
        scratch_shapes=[pltpu.VMEM((D // 2, 2 * rows), bf16), pltpu.VMEM((2 * rows, D // 2), bf16)],
        compiler_params=pltpu.CompilerParams(vmem_limit_bytes=48 * 2**20),
        name="partial_sums",
    )(core, embeddings, other, rotation, centroids, words, other_words)
    arrived = lax.all_to_all(parts, "x", split_axis=0, concat_axis=0, tiled=True)
    pieces = pl.pallas_call(
        first_sums,
        out_shape=jax.ShapeDtypeStruct((peers, CHUNK, LANES), bf16),
        in_specs=[VMEM],
        out_specs=VMEM,
        scratch_shapes=[pltpu.VMEM((ROWS, LANES), f32)],
        name="first_sums",
    )(arrived)
    arrived = lax.all_to_all(pieces, DP, split_axis=0, concat_axis=0, tiled=True)
    coarse_sums, mine = pl.pallas_call(
        lambda *refs: owned_sums(*refs, vectors=vectors),
        out_shape=(
            jax.ShapeDtypeStruct((1, LANES), f32),
            jax.ShapeDtypeStruct((CHUNK, LANES), f32),
        ),
        in_specs=[SMEM, VMEM],
        out_specs=(VMEM, VMEM),
        name="owned_sums",
    )(place, arrived)
    spread = jnp.broadcast_to(mine.astype(f16)[None], (peers, CHUNK, LANES))
    arrived = lax.all_to_all(spread, DP, split_axis=0, concat_axis=0, tiled=True)
    gram, codebook_sums = pl.pallas_call(
        laid_out,
        out_shape=(jax.ShapeDtypeStruct((LANES, D), f32), jax.ShapeDtypeStruct((K, LANES), f32)),
        in_specs=[VMEM],
        out_specs=(VMEM, VMEM),
        scratch_shapes=[pltpu.VMEM((COARSE0, LANES), f32)],
        name="laid_out",
    )(arrived.astype(f32))
    return gram, coarse_sums, codebook_sums


def solution(mesh):
    finer = Mesh(mesh.devices.reshape(12, 8, X, 2), DP_SUB)
    return jax.shard_map(
        per_device,
        mesh=finer,
        in_specs=(P(DP_SUB, None), P(), P(), P(DP_SUB), P(DP_SUB, None)),
        out_specs=(P(("x", "c"), None), P(DP, ("x", "c")), P(None, ("x", "c"))),
        check_vma=False,
    )
```

time: 319 us -> 125 us (0.39)
  the two profiles are of different devices: /device:TPU:4 before, /device:TPU:8 now
where the time goes in v1:
time: 125 us; the launch traced here: 124 us
  blocking collectives  51.5 us (41%)
  starting transfers between devices  26.1 us (21%)
  waiting for transfers between devices  23.2 us (19%)
  Pallas kernels  14.7 us (12%)
  local copies, waits for them, and re-layouts  5.23 us (4%)
  other arithmetic  2.55 us (2%)
    all_to_all x1, blocking collectives, per_device(): lax.all_to_all(spread, DP, split_axis=0, concat_axis=0, tiled=True)  27.8 us
    all_to_all x1, blocking collectives, per_device(): lax.all_to_all(parts, 'x', split_axis=0, concat_axis=0, tiled=True)  23.7 us
    all_to_all x1, waiting for transfers between devices, per_device(): lax.all_to_all(pieces, DP, split_axis=0, concat_axis=0, tiled=True)  22.2 us
    all_to_all x1, starting transfers between devices, per_device(): lax.all_to_all(pieces, DP, split_axis=0, concat_axis=0, tiled=True)  21.8 us
    pallas_call x1, Pallas kernels, per_device(): pl.pallas_call(partial_sums, out_shape=jax.ShapeDtypeStruct((X, ROWS, LAN...  8.43 us
    unnamed x8, local copies, waits for them, and re-layouts  4.49 us
  transfers between devices with their start and end apart: 3, of which 2 were waited for; matrix products, arithmetic and copies ran while one was open for 1% of the time, Pallas kernels for 0%

profile of v1, /device:TPU:8, one launch (start us, length us, event | category | flops | bytes accessed | tf_op | source)
XLA Modules:
  0.0 124.0 jit_solution(1912010756971893205)
XLA Ops:
  0.6 1.9 %collective-permute-start = (bf16[512,1024]{1,0:T(8,128)(2,1)}, bf16[512,1024]{1,0:T(8,128)(2,1)S(1)}, u32[]{:S(2)}, u32[]{:S(2)}) collective-permute-start(bf16[512,1024]{1,0:T(8,128)(2,1)} %e0.1), channel_id=1, source_target_pairs={{0,1},{1,0},{2,3},{3,2},{4,5},{5,4},{6,7},{7,6},{8,9},{9,8},{10,11... | collective-permute-start | bytes 3145736 | tf_op jit(solution)/shard_map/ppermute | solution.py:138
  2.6 0.7 broadcast_in_dim.4
  3.2 0.9 pad_add_fusion.p0
  4.2 2.4 %collective-permute-start.1 = (s32[72,512]{1,0:T(8,128)S(1)}, s32[72,512]{1,0:T(8,128)S(1)}, u32[]{:S(2)}, u32[]{:S(2)}) collective-permute-start(s32[72,512]{1,0:T(8,128)S(1)} %pad_add_fusion.p0), channel_id=1, source_target_pairs={{0,1},{1,0},{2,3},{3,2},{4,5},{5,4},{6,7},{7,6},{8,9},{9,8},{10,11... | collective-permute-start | bytes 442376 | tf_op jit(solution)/shard_map/ppermute | solution.py:139
  6.6 1.0 collective-permute-done.1.p1
  7.6 0.0 collective-permute-done.e1
  7.6 0.0 copy-start
  7.6 1.6 %copy-done = bf16[1024,1024]{1,0:T(8,128)(2,1)S(1)} copy-done((bf16[1024,1024]{1,0:T(8,128)(2,1)S(1)}, bf16[1024,1024]{1,0:T(8,128)(2,1)}, u32[]{:S(2)}) %copy-start) | copy-done | bytes 2097176
  9.2 0.0 copy-start.1
  9.2 1.2 copy-done.1
  10.4 0.0 copy-start.2
  10.4 0.9 copy-done.2
  11.3 8.4 %partial_sums.1 = bf16[4,1376,128]{2,1,0:T(8,128)(2,1)S(1)} custom-call(s32[1]{0:T(128)} %bitcast.1.core_ref, bf16[512,1024]{1,0:T(8,128)(2,1)S(1)} %copy-done.1, bf16[512,1024]{1,0:T(8,128)(2,1)S(1)} %collective-permute-done.e1, bf16[1024,1024]{1,0:T(8,128)(2,1)S(1)} %copy-done, bf16[96,1024]{1,0:T(8,128)(2,1)S(1)} %copy-done.2, ...), custom_call_target="tpu_custom_call" | custom-call | tf_op jit(solution)/shard_map/partial_sums/pallas_call | solution.py:140
  19.7 23.7 %all_to_all.15.arrived = bf16[4,1376,128]{2,1,0:T(8,128)(2,1)} all-to-all(bf16[4,1376,128]{2,1,0:T(8,128)(2,1)S(1)} %partial_sums.1), channel_id=1, replica_groups=mesh['z'=12,'y'=8,'x'=4,'c'=2] {'x'}, dimensions={0} | all-to-all | bytes 2818048 | tf_op jit(solution)/shard_map/all_to_all | solution.py:149
  43.4 2.4 %first_sums.1 = bf16[96,16,128]{2,1,0:T(8,128)(2,1)} custom-call(bf16[4,1376,128]{2,1,0:T(8,128)(2,1)} %all_to_all.15.arrived), custom_call_target="tpu_custom_call" | custom-call | tf_op jit(solution)/shard_map/first_sums/pallas_call | solution.py:150
  45.8 21.8 %all-to-all-start.1 = ((bf16[96,16,128]{2,1,0:T(8,128)(2,1)}), bf16[96,16,128]{2,1,0:T(8,128)(2,1)S(1)}, u32[]{:S(2)}, u32[]{:S(2)}) async-start(bf16[96,16,128]{2,1,0:T(8,128)(2,1)} %first_sums.1), calls=%async_computation.1 | async-start | bytes 786432 | tf_op jit(solution)/shard_map/all_to_all | solution.py:158
  67.6 22.2 %all-to-all-done.1.refs_1_ = bf16[96,16,128]{2,1,0:T(8,128)(2,1)S(1)} async-done(((bf16[96,16,128]{2,1,0:T(8,128)(2,1)}), bf16[96,16,128]{2,1,0:T(8,128)(2,1)S(1)}, u32[]{:S(2)}, u32[]{:S(2)}) %all-to-all-start.1) | async-done | bytes 393248 | tf_op jit(solution)/shard_map/all_to_all | solution.py:158
  89.9 0.0 copy-start.3
  89.9 0.7 copy-done.3
  90.6 1.8 %owned_sums.1 = (f32[1,128]{1,0:T(1,128)}, f32[16,128]{1,0:T(8,128)}) custom-call(s32[1]{0:T(128)} %bitcast.refs_0_, bf16[96,16,128]{2,1,0:T(8,128)(2,1)} %copy-done.3), custom_call_target="tpu_custom_call" | custom-call | tf_op jit(solution)/shard_map/owned_sums/pallas_call | solution.py:159
  92.4 0.7 convert_element_type.6
  93.1 0.1 broadcast_in_dim.5
  93.2 27.8 %all_to_all.16 = f16[96,16,128]{2,1,0:T(8,128)(2,1)S(1)} all-to-all(f16[96,16,128]{2,1,0:T(8,128)(2,1)S(1)} %broadcast_in_dim.5), channel_id=1, replica_groups=mesh['z'=12,'y'=8,'x'=4,'c'=2] {'z','y'}, dimensions={0} | all-to-all | bytes 786432 | tf_op jit(solution)/shard_map/all_to_all | solution.py:170
  121.0 0.9 convert_element_type.7.arrived
  121.9 2.1 %laid_out.1 = (f32[128,1024]{1,0:T(8,128)}, f32[256,128]{1,0:T(8,128)}) custom-call(f32[96,16,128]{2,1,0:T(8,128)} %convert_element_type.7.arrived), custom_call_target="tpu_custom_call" | custom-call | tf_op jit(solution)/shard_map/laid_out/pallas_call | solution.py:171
Async XLA Ops:
  0.6 6.9 %collective-permute-start = (bf16[512,1024]{1,0:T(8,128)(2,1)}, bf16[512,1024]{1,0:T(8,128)(2,1)S(1)}, u32[]{:S(2)}, u32[]{:S(2)}) collective-permute-start(bf16[512,1024]{1,0:T(8,128)(2,1)} %e0.1), channel_id=1, source_target_pairs={{0,1},{1,0},{2,3},{3,2},{4,5},{5,4},{6,7},{7,6},{8,9},{9,8},{10,11... | collective-permute-start | bytes 3145736 | tf_op jit(solution)/shard_map/ppermute | solution.py:138
  4.2 3.4 %collective-permute-start.1 = (s32[72,512]{1,0:T(8,128)S(1)}, s32[72,512]{1,0:T(8,128)S(1)}, u32[]{:S(2)}, u32[]{:S(2)}) collective-permute-start(s32[72,512]{1,0:T(8,128)S(1)} %pad_add_fusion.p0), channel_id=1, source_target_pairs={{0,1},{1,0},{2,3},{3,2},{4,5},{5,4},{6,7},{7,6},{8,9},{9,8},{10,11... | collective-permute-start | bytes 442376 | tf_op jit(solution)/shard_map/ppermute | solution.py:139
  7.6 1.6 %copy-start = (bf16[1024,1024]{1,0:T(8,128)(2,1)S(1)}, bf16[1024,1024]{1,0:T(8,128)(2,1)}, u32[]{:S(2)}) copy-start(bf16[1024,1024]{1,0:T(8,128)(2,1)} %rot.1) | copy-start | bytes 6291460
  9.2 1.2 copy-start.1
  10.4 0.9 copy-start.2
  45.8 44.0 %all-to-all-start.1 = ((bf16[96,16,128]{2,1,0:T(8,128)(2,1)}), bf16[96,16,128]{2,1,0:T(8,128)(2,1)S(1)}, u32[]{:S(2)}, u32[]{:S(2)}) async-start(bf16[96,16,128]{2,1,0:T(8,128)(2,1)} %first_sums.1), calls=%async_computation.1 | async-start | bytes 786432 | tf_op jit(solution)/shard_map/all_to_all | solution.py:158
  89.9 0.7 copy-start.3

commit v2 on v1

v2 whole, which is shorter than its diff:
```python
import jax
import jax.numpy as jnp
from jax import lax
from jax.experimental import pallas as pl
from jax.experimental.pallas import tpu as pltpu
from jax.sharding import Mesh
from jax.sharding import PartitionSpec as P

D = 1024
M = 64
K = 256
CENTS = 96
LANES = 128
X = 4
Y = 8
ZF = 2
ZS = 6
OWNERS = ("zf", "y")
PEERS = ZF * Y
DP = ("zs", "zf", "y")
DP_SUB = ("zs", "zf", "y", "x", "c")
BOOK0 = D
COARSE0 = D + K
ROWS = D + K + CENTS
GP = D // PEERS
BP = K // PEERS
CP = CENTS // PEERS
C0 = GP + BP
PART = C0 + 16
ONE = PART + BP
SPREAD = C0 + 8
bf16 = jnp.bfloat16
f16 = jnp.float16
f32 = jnp.float32
VMEM = pl.BlockSpec(memory_space=pltpu.VMEM)
SMEM = pl.BlockSpec(memory_space=pltpu.SMEM)


def params(mib):
    return pltpu.CompilerParams(vmem_limit_bytes=mib * 2**20)


def dot(a, b):
    return jnp.dot(a, b, preferred_element_type=f32)


def partial_sums(core_ref, place_ref, e0, e1, rot, cent, p0, p1, out, turned, res):
    core = core_ref[0]
    rows = e0.shape[0]
    halves = ((e0, p0), (e1, p1))

    def columns(x):
        return pl.ds(pl.multiple_of((2 * x + core) * LANES, LANES), LANES)

    for x in range(X):
        for h, (e, _) in enumerate(halves):
            turned[x * LANES : (x + 1) * LANES, h * rows : (h + 1) * rows] = e[:, columns(x)].T
    wide = 256
    for n in range(D // wide):
        cols = slice(n * wide, (n + 1) * wide)
        g = dot(turned[:, :rows], e0[:, cols]) + dot(turned[:, rows:], e1[:, cols])
        for x in range(X):
            for k in range(wide // LANES):
                j = n * (wide // LANES) + k
                out[x, j * LANES : (j + 1) * LANES, :] = g[
                    x * LANES : (x + 1) * LANES, k * LANES : (k + 1) * LANES
                ].astype(bf16)

    label = lax.broadcasted_iota(jnp.int32, (CENTS, rows), 0)
    per_zf = CENTS // ZF
    sent = ((label % CP) * ZF + label // per_zf) * Y + (label // CP) % Y
    picks = [(label == p[M : M + 1, :]).astype(bf16) for _, p in halves]
    sends = [(sent == p[M : M + 1, :]).astype(bf16) for _, p in halves]
    for q in range(X // 2):
        r = jnp.concatenate([rot[:, columns(2 * q)], rot[:, columns(2 * q + 1)]], axis=1)
        c = jnp.concatenate([cent[:, columns(2 * q)], cent[:, columns(2 * q + 1)]], axis=1)
        coarse = jnp.zeros((CENTS, 2 * LANES), f32)
        for h, (e, _) in enumerate(halves):
            base = lax.dot_general(picks[h], c, (((0,), (0,)), ((), ())), preferred_element_type=f32)
            residual = (dot(e[...], r) - base).astype(bf16)
            res[h * rows : (h + 1) * rows, q * 2 * LANES : (q + 1) * 2 * LANES] = residual
            coarse += dot(sends[h], residual)
        for k in range(2):
            out[2 * q + k, COARSE0:ROWS, :] = coarse[:, k * LANES : (k + 1) * LANES].astype(bf16)

    word = lax.broadcasted_iota(jnp.int32, (K, rows), 0)
    lane = lax.broadcasted_iota(jnp.int32, (rows, LANES), 1)
    subs = M // 8

    def book(x, carry):
        total = jnp.zeros((K, LANES), f32)
        for h, (_, p) in enumerate(halves):
            first = pl.multiple_of((2 * x + core) * subs, subs)
            codes = p[pl.ds(first, subs), :]
            mine = res[h * rows : (h + 1) * rows, pl.ds(pl.multiple_of(x * LANES, LANES), LANES)]
            for m in range(subs):
                onehot = (word == codes[m : m + 1, :]).astype(bf16)
                part = jnp.where(lane // (LANES // subs) == m, mine, jnp.zeros_like(mine))
                total += dot(onehot, part)
        out[x, BOOK0:COARSE0, :] = total.astype(bf16)
        return carry

    lax.fori_loop(0, X, book, 0)


def first_sums(arrived, out):
    def summed(a, b):
        return arrived[:, a:b, :].astype(f32).sum(axis=0)

    coarse = summed(COARSE0, ROWS)
    zeros = jnp.zeros((PART - C0 - CP, LANES), f32)
    for q in range(PEERS):
        out[q, :GP, :] = summed(q * GP, (q + 1) * GP).astype(bf16)
        out[q, GP:C0, :] = summed(BOOK0 + q * BP, BOOK0 + (q + 1) * BP).astype(bf16)
        mine = coarse[q * CP : (q + 1) * CP, :]
        out[q, C0:PART, :] = jnp.concatenate([mine, zeros], axis=0).astype(bf16)


def second_sums(arrived, out):
    total = arrived[...].astype(f32).sum(axis=0)
    high = total.astype(bf16)
    low = total - high.astype(f32)
    coarse = jnp.concatenate([total[C0 : C0 + 8], low[C0 : C0 + 8]], axis=0).astype(bf16)
    book = low[GP:C0].astype(bf16)
    for i in range(out.shape[0]):
        out[i, :C0, :] = high[:C0]
        out[i, C0:PART, :] = coarse
        out[i, PART:ONE, :] = book


def owned_sums(place_ref, arrived, coarse_out, mine, *, vectors):
    total = arrived[...].astype(f32).sum(axis=0)
    coarse = total[C0 : C0 + 8] + total[C0 + 8 : C0 + 16]
    row = lax.broadcasted_iota(jnp.int32, (8, LANES), 0)
    own = jnp.where(row == place_ref[0], coarse, 0.0).sum(axis=0, keepdims=True)
    coarse_out[...] = own * (CENTS / vectors) ** 0.5
    gram = total[:GP] * (1.0 / vectors)
    book = (total[GP:C0] + total[PART:ONE]) * (K / vectors) ** 0.5

    def scaled(v):
        top = jnp.max(jnp.abs(v), keepdims=True)
        power = jnp.ceil(jnp.log2(jnp.maximum(top, 2.0**-100)))
        return v * jnp.exp2(-power), jnp.broadcast_to(power, (8, LANES))

    gram, gram_power = scaled(gram)
    book, book_power = scaled(book)
    mine[:GP, :] = gram
    mine[GP:C0, :] = book
    mine[C0:SPREAD, :] = jnp.where(row == 0, gram_power, book_power)


def laid_out(arrived, gram, book):
    for q in range(PEERS):
        power = jnp.exp2(arrived[q, C0:SPREAD, :])
        j, top = q * GP // LANES, q * GP % LANES
        gram[top : top + GP, j * LANES : (j + 1) * LANES] = arrived[q, :GP, :] * power[0:1]
        book[q * BP : (q + 1) * BP, :] = arrived[q, GP:C0, :] * power[1:2]


def per_device(embeddings, rotation, centroids, assignments, codes):
    rows = embeddings.shape[0]
    vectors = rows * lax.axis_size(DP_SUB)
    core = lax.axis_index("c").reshape(1)
    place = lax.axis_index("zs").reshape(1)
    words = jnp.concatenate([codes.T, jnp.broadcast_to(assignments[None, :], (8, rows))], axis=0)
    swap = [(0, 1), (1, 0)]
    other = lax.ppermute(embeddings, "c", swap)
    other_words = lax.ppermute(words, "c", swap)
    parts = pl.pallas_call(
        partial_sums,
        out_shape=jax.ShapeDtypeStruct((X, ROWS, LANES), bf16),
        in_specs=[SMEM] * 2 + [VMEM] * 6,
        out_specs=VMEM,
        scratch_shapes=[pltpu.VMEM((D // 2, 2 * rows), bf16), pltpu.VMEM((2 * rows, D // 2), bf16)],
        compiler_params=params(32),
        name="partial_sums",
    )(core, place, embeddings, other, rotation, centroids, words, other_words)
    arrived = lax.all_to_all(parts, "x", split_axis=0, concat_axis=0, tiled=True)
    pieces = pl.pallas_call(
        first_sums,
        out_shape=jax.ShapeDtypeStruct((PEERS, PART, LANES), bf16),
        in_specs=[VMEM],
        out_specs=VMEM,
        compiler_params=params(16),
        name="first_sums",
    )(arrived)
    arrived = lax.all_to_all(pieces, OWNERS, split_axis=0, concat_axis=0, tiled=True)
    pieces = pl.pallas_call(
        second_sums,
        out_shape=jax.ShapeDtypeStruct((ZS, ONE, LANES), bf16),
        in_specs=[VMEM],
        out_specs=VMEM,
        compiler_params=params(16),
        name="second_sums",
    )(arrived)
    arrived = lax.all_to_all(pieces, "zs", split_axis=0, concat_axis=0, tiled=True)
    coarse_sums, mine = pl.pallas_call(
        lambda *refs: owned_sums(*refs, vectors=vectors),
        out_shape=(
            jax.ShapeDtypeStruct((1, LANES), f32),
            jax.ShapeDtypeStruct((SPREAD, LANES), f32),
        ),
        in_specs=[SMEM, VMEM],
        out_specs=(VMEM, VMEM),
        compiler_params=params(16),
        name="owned_sums",
    )(place, arrived)
    spread = jnp.broadcast_to(mine.astype(f16)[None], (PEERS, SPREAD, LANES))
    arrived = lax.all_to_all(spread, OWNERS, split_axis=0, concat_axis=0, tiled=True)
    gram, codebook_sums = pl.pallas_call(
        laid_out,
        out_shape=(jax.ShapeDtypeStruct((LANES, D), f32), jax.ShapeDtypeStruct((K, LANES), f32)),
        in_specs=[VMEM],
        out_specs=(VMEM, VMEM),
        compiler_params=params(16),
        name="laid_out",
    )(arrived.astype(f32))
    return gram, coarse_sums, codebook_sums


def solution(mesh):
    finer = Mesh(mesh.devices.reshape(ZS, ZF, Y, X, 2), DP_SUB)
    return jax.shard_map(
        per_device,
        mesh=finer,
        in_specs=(P(DP_SUB, None), P(), P(), P(DP_SUB), P(DP_SUB, None)),
        out_specs=(P(("x", "c"), None), P(DP, ("x", "c")), P(None, ("x", "c"))),
        check_vma=False,
    )
```

time: 125 us -> 107 us (0.86)
  blocking collectives: 51.5 us -> 84.8 us
  waiting for transfers between devices: 23.2 us -> 0.98 us
  starting transfers between devices: 26.1 us -> 4.33 us
  Pallas kernels: 14.7 us -> 10.1 us
  other arithmetic: 2.55 us -> 0.97 us
    all_to_all x1 -> x3, blocking collectives: 27.8 us -> 61.2 us  [the longest x1 23.3 us: per_device(): lax.all_to_all(pieces, 'zs', split_axis=0, concat_axis=0, tiled=True)]
    all_to_all x1 -> x0, waiting for transfers between devices: 22.2 us -> none  [per_device(): lax.all_to_all(pieces, DP, split_axis=0, concat_axis=0, tiled=True)]
    all_to_all x1 -> x0, starting transfers between devices: 21.8 us -> none  [per_device(): lax.all_to_all(pieces, DP, split_axis=0, concat_axis=0, tiled=True)]
    pallas_call x1 -> x2, Pallas kernels: 2.41 us -> 0.24 us  [the longest x1 0.18 us: per_device(): pl.pallas_call(first_sums, out_shape=jax.ShapeDtypeStruct((PEERS, PART, L...]
    pallas_call x1, Pallas kernels: 1.83 us -> 0.54 us  [per_device(): pl.pallas_call(lambda *refs: owned_sums(*refs, vectors=vectors), out_shap...]
    unnamed x8 -> x6, local copies, waits for them, and re-layouts: 4.49 us -> 3.74 us
  transfers between devices with their start and end apart: 3 -> 2, of which waited for: 2 -> 1; matrix products, arithmetic and copies ran while one was open for 1% -> 2% of each run, Pallas kernels for 0% -> 0%
where the time goes in v2:
time: 107 us; the launch traced here: 106 us
  blocking collectives  84.8 us (79%)
  Pallas kernels  10.1 us (9%)
  local copies, waits for them, and re-layouts  4.48 us (4%)
  starting transfers between devices  4.33 us (4%)
    all_to_all x1, blocking collectives, per_device(): lax.all_to_all(parts, 'x', split_axis=0, concat_axis=0, tiled=True)  23.6 us
    all_to_all x1, blocking collectives, per_device(): lax.all_to_all(pieces, 'zs', split_axis=0, concat_axis=0, tiled=True)  23.3 us
    all_to_all x1, blocking collectives, per_device(): lax.all_to_all(pieces, OWNERS, split_axis=0, concat_axis=0, tiled=True)  23 us
    all_to_all x1, blocking collectives, per_device(): lax.all_to_all(spread, OWNERS, split_axis=0, concat_axis=0, tiled=True)  14.9 us
    pallas_call x1, Pallas kernels, per_device(): pl.pallas_call(partial_sums, out_shape=jax.ShapeDtypeStruct((X, ROWS, LAN...  8.45 us
    unnamed x6, local copies, waits for them, and re-layouts  3.74 us
    ppermute x1, starting transfers between devices, per_device(): other_words = lax.ppermute(words, 'c', swap)  2.41 us
  transfers between devices with their start and end apart: 2, of which 1 were waited for; matrix products, arithmetic and copies ran while one was open for 2% of the time, Pallas kernels for 0%

profile of v2, /device:TPU:8, one launch (start us, length us, event | category | flops | bytes accessed | tf_op | source)
XLA Modules:
  0.0 106.4 jit_solution(15305943644141263142)
XLA Ops:
  0.6 1.9 %collective-permute-start = (bf16[512,1024]{1,0:T(8,128)(2,1)}, bf16[512,1024]{1,0:T(8,128)(2,1)S(1)}, u32[]{:S(2)}, u32[]{:S(2)}) collective-permute-start(bf16[512,1024]{1,0:T(8,128)(2,1)} %e0.1), channel_id=1, source_target_pairs={{0,1},{1,0},{2,3},{3,2},{4,5},{5,4},{6,7},{7,6},{8,9},{9,8},{10,11... | collective-permute-start | bytes 3145736 | tf_op jit(solution)/shard_map/ppermute | solution.py:167
  2.6 0.7 broadcast_in_dim.4
  3.2 0.9 pad_add_fusion.p0
  4.2 2.4 %collective-permute-start.1 = (s32[72,512]{1,0:T(8,128)S(1)}, s32[72,512]{1,0:T(8,128)S(1)}, u32[]{:S(2)}, u32[]{:S(2)}) collective-permute-start(s32[72,512]{1,0:T(8,128)S(1)} %pad_add_fusion.p0), channel_id=1, source_target_pairs={{0,1},{1,0},{2,3},{3,2},{4,5},{5,4},{6,7},{7,6},{8,9},{9,8},{10,11... | collective-permute-start | bytes 442376 | tf_op jit(solution)/shard_map/ppermute | solution.py:168
  6.6 1.0 collective-permute-done.1.p1
  7.6 0.0 collective-permute-done.e1
  7.6 0.0 copy-start
  7.6 1.6 %copy-done = bf16[1024,1024]{1,0:T(8,128)(2,1)S(1)} copy-done((bf16[1024,1024]{1,0:T(8,128)(2,1)S(1)}, bf16[1024,1024]{1,0:T(8,128)(2,1)}, u32[]{:S(2)}) %copy-start) | copy-done | bytes 2097176
  9.2 0.0 copy-start.1
  9.2 1.2 %copy-done.1 = bf16[512,1024]{1,0:T(8,128)(2,1)S(1)} copy-done((bf16[512,1024]{1,0:T(8,128)(2,1)S(1)}, bf16[512,1024]{1,0:T(8,128)(2,1)}, u32[]{:S(2)}) %copy-start.1) | copy-done | bytes 1048600
  10.4 0.0 copy-start.2
  10.4 0.9 copy-done.2
  11.3 8.4 %partial_sums.1 = bf16[4,1376,128]{2,1,0:T(8,128)(2,1)S(1)} custom-call(s32[1]{0:T(128)} %bitcast.1.core_ref, s32[1]{0:T(128)} %bitcast.place_ref.refs_0_, bf16[512,1024]{1,0:T(8,128)(2,1)S(1)} %copy-done.1, bf16[512,1024]{1,0:T(8,128)(2,1)S(1)} %collective-permute-done.e1, bf16[1024,1024]{1,0:T(8,128)(2,1)S(1)} %copy-done, bf16[96,1024]{1,0:T(8,128)(2,1)S(1)} %copy-done.2, ...), custom_call_target="tpu_custom_call" | custom-call | tf_op jit(solution)/shard_map/partial_sums/pallas_call | solution.py:169
  19.8 23.6 %all_to_all.20.arrived = bf16[4,1376,128]{2,1,0:T(8,128)(2,1)S(1)} all-to-all(bf16[4,1376,128]{2,1,0:T(8,128)(2,1)S(1)} %partial_sums.1), channel_id=1, replica_groups=mesh['zs'=6,'zf'=2,'y'=8,'x'=4,'c'=2] {'x'}, dimensions={0} | all-to-all | bytes 2818048 | tf_op jit(solution)/shard_map/all_to_all | solution.py:178
  43.3 0.2 first_sums.1
  43.5 23.0 %all_to_all.21.arrived = bf16[16,96,128]{2,1,0:T(8,128)(2,1)S(1)} all-to-all(bf16[16,96,128]{2,1,0:T(8,128)(2,1)S(1)} %first_sums.1), channel_id=1, replica_groups=mesh['zs'=6,'zf'=2,'y'=8,'x'=4,'c'=2] {'zf','y'}, dimensions={0} | all-to-all | bytes 786432 | tf_op jit(solution)/shard_map/all_to_all | solution.py:187
  66.6 0.1 second_sums.1
  66.6 23.3 %all_to_all.22.refs_1_ = bf16[6,112,128]{2,1,0:T(8,128)(2,1)S(1)} all-to-all(bf16[6,112,128]{2,1,0:T(8,128)(2,1)S(1)} %second_sums.1), channel_id=1, replica_groups=mesh['zs'=6,'zf'=2,'y'=8,'x'=4,'c'=2] {'zs'}, dimensions={0} | all-to-all | bytes 344064 | tf_op jit(solution)/shard_map/all_to_all | solution.py:196
  89.9 0.5 owned_sums.1
  90.5 0.1 broadcast_in_dim.5
  90.5 14.9 %all_to_all.23 = f16[16,88,128]{2,1,0:T(8,128)(2,1)S(1)} all-to-all(f16[16,88,128]{2,1,0:T(8,128)(2,1)S(1)} %broadcast_in_dim.5), channel_id=1, replica_groups=mesh['zs'=6,'zf'=2,'y'=8,'x'=4,'c'=2] {'zf','y'}, dimensions={0} | all-to-all | bytes 720896 | tf_op jit(solution)/shard_map/all_to_all | solution.py:209
  105.5 0.9 laid_out.1
  (2 shorter events, 0.1 us)
Async XLA Ops:
  0.6 6.9 %collective-permute-start = (bf16[512,1024]{1,0:T(8,128)(2,1)}, bf16[512,1024]{1,0:T(8,128)(2,1)S(1)}, u32[]{:S(2)}, u32[]{:S(2)}) collective-permute-start(bf16[512,1024]{1,0:T(8,128)(2,1)} %e0.1), channel_id=1, source_target_pairs={{0,1},{1,0},{2,3},{3,2},{4,5},{5,4},{6,7},{7,6},{8,9},{9,8},{10,11... | collective-permute-start | bytes 3145736 | tf_op jit(solution)/shard_map/ppermute | solution.py:167
  4.2 3.4 %collective-permute-start.1 = (s32[72,512]{1,0:T(8,128)S(1)}, s32[72,512]{1,0:T(8,128)S(1)}, u32[]{:S(2)}, u32[]{:S(2)}) collective-permute-start(s32[72,512]{1,0:T(8,128)S(1)} %pad_add_fusion.p0), channel_id=1, source_target_pairs={{0,1},{1,0},{2,3},{3,2},{4,5},{5,4},{6,7},{7,6},{8,9},{9,8},{10,11... | collective-permute-start | bytes 442376 | tf_op jit(solution)/shard_map/ppermute | solution.py:168
  7.6 1.6 %copy-start = (bf16[1024,1024]{1,0:T(8,128)(2,1)S(1)}, bf16[1024,1024]{1,0:T(8,128)(2,1)}, u32[]{:S(2)}) copy-start(bf16[1024,1024]{1,0:T(8,128)(2,1)} %rot.1) | copy-start | bytes 6291460
  9.2 1.2 %copy-start.1 = (bf16[512,1024]{1,0:T(8,128)(2,1)S(1)}, bf16[512,1024]{1,0:T(8,128)(2,1)}, u32[]{:S(2)}) copy-start(bf16[512,1024]{1,0:T(8,128)(2,1)} %e0.1) | copy-start | bytes 3145732
  10.4 0.9 copy-start.2

commit v3 on v2

--- a/solution.py
+++ b/solution.py
@@ -11,6 +11,7 @@
 K = 256
 CENTS = 96
 LANES = 128
+SUBS = 8
 X = 4
 Y = 8
 ZF = 2
@@ -34,6 +35,7 @@
 f32 = jnp.float32
 VMEM = pl.BlockSpec(memory_space=pltpu.VMEM)
 SMEM = pl.BlockSpec(memory_space=pltpu.SMEM)
+HBM = pl.BlockSpec(memory_space=pltpu.HBM)
 
 
 def params(mib):
@@ -44,17 +46,87 @@
     return jnp.dot(a, b, preferred_element_type=f32)
 
 
-def partial_sums(core_ref, place_ref, e0, e1, rot, cent, p0, p1, out, turned, res):
+def columns(core, x):
+    return pl.ds(pl.multiple_of((2 * x + core) * LANES, LANES), LANES)
+
+
+def residual_sums(e, rot, cent, assigned, codes_of, res, add):
+    rows = e.shape[0]
+    label = lax.broadcasted_iota(jnp.int32, (CENTS, rows), 0)
+    per_zf = CENTS // ZF
+    sent = ((label % CP) * ZF + label // per_zf) * Y + (label // CP) % Y
+    pick = (label == assigned).astype(bf16)
+    send = (sent == assigned).astype(bf16)
+    for q in range(X // 2):
+        pair = slice(q * 2 * LANES, (q + 1) * 2 * LANES)
+        base = lax.dot_general(
+            pick, cent[:, pair], (((0,), (0,)), ((), ())), preferred_element_type=f32
+        )
+        residual = (dot(e[...], rot[:, pair]) - base).astype(bf16)
+        res[:, pair] = residual
+        coarse = dot(send, residual)
+        for k in range(2):
+            add(2 * q + k, K, CENTS, coarse[:, k * LANES : (k + 1) * LANES])
+    word = lax.broadcasted_iota(jnp.int32, (K, rows), 0)
+    lane = lax.broadcasted_iota(jnp.int32, (rows, LANES), 1)
+
+    def book(x, carry):
+        codes = codes_of(x)
+        mine = res[:, pl.ds(pl.multiple_of(x * LANES, LANES), LANES)]
+        total = jnp.zeros((K, LANES), f32)
+        for m in range(SUBS):
+            onehot = (word == codes[m : m + 1, :]).astype(bf16)
+            part = jnp.where(lane // (LANES // SUBS) == m, mine, jnp.zeros_like(mine))
+            total += dot(onehot, part)
+        add(x, 0, K, total)
+        return carry
+
+    lax.fori_loop(0, X, book, 0)
+
+
+def own_sums(
+    core_ref, place_ref, e_in, rot_in, cent_in, codes_in, assigned_in,
+    sums, words, e, rot, cent, codes, assigned_ref, res, sems,
+):
+    core = core_ref[0]
+    copies = [
+        pltpu.make_async_copy(assigned_in, assigned_ref, sems.at[0]),
+        pltpu.make_async_copy(codes_in, codes, sems.at[1]),
+        pltpu.make_async_copy(e_in, e, sems.at[2]),
+    ]
+    for x in range(X):
+        here = slice(x * LANES, (x + 1) * LANES)
+        for source, target, k in ((cent_in, cent, 0), (rot_in, rot, X)):
+            copies.append(
+                pltpu.make_async_copy(
+                    source.at[:, columns(core, x)], target.at[:, here], sems.at[3 + k + x]
+                )
+            )
+    for copy in copies:
+        copy.start()
+    for copy in copies:
+        copy.wait()
+    assigned = assigned_ref[...].reshape(1, -1)
+
+    def rows_of(x, whose):
+        return pl.ds(pl.multiple_of((2 * x + whose) * SUBS, SUBS), SUBS)
+
+    for x in range(X):
+        words[x * SUBS : (x + 1) * SUBS, :] = codes[rows_of(x, 1 - core), :]
+    words[X * SUBS :, :] = jnp.broadcast_to(assigned, (SUBS, assigned.shape[1]))
+
+    def add(x, start, size, value):
+        sums[x, start : start + size, :] = value
+
+    residual_sums(e, rot, cent, assigned, lambda x: codes[rows_of(x, core), :], res, add)
+
+
+def partial_sums(core_ref, e0, e1, rot, cent, words, sums, out, turned, res):
     core = core_ref[0]
     rows = e0.shape[0]
-    halves = ((e0, p0), (e1, p1))
-
-    def columns(x):
-        return pl.ds(pl.multiple_of((2 * x + core) * LANES, LANES), LANES)
-
     for x in range(X):
-        for h, (e, _) in enumerate(halves):
-            turned[x * LANES : (x + 1) * LANES, h * rows : (h + 1) * rows] = e[:, columns(x)].T
+        for h, e in enumerate((e0, e1)):
+            turned[x * LANES : (x + 1) * LANES, h * rows : (h + 1) * rows] = e[:, columns(core, x)].T
     wide = 256
     for n in range(D // wide):
         cols = slice(n * wide, (n + 1) * wide)
@@ -66,41 +138,15 @@
                     x * LANES : (x + 1) * LANES, k * LANES : (k + 1) * LANES
                 ].astype(bf16)
 
-    label = lax.broadcasted_iota(jnp.int32, (CENTS, rows), 0)
-    per_zf = CENTS // ZF
-    sent = ((label % CP) * ZF + label // per_zf) * Y + (label // CP) % Y
-    picks = [(label == p[M : M + 1, :]).astype(bf16) for _, p in halves]
-    sends = [(sent == p[M : M + 1, :]).astype(bf16) for _, p in halves]
-    for q in range(X // 2):
-        r = jnp.concatenate([rot[:, columns(2 * q)], rot[:, columns(2 * q + 1)]], axis=1)
-        c = jnp.concatenate([cent[:, columns(2 * q)], cent[:, columns(2 * q + 1)]], axis=1)
-        coarse = jnp.zeros((CENTS, 2 * LANES), f32)
-        for h, (e, _) in enumerate(halves):
-            base = lax.dot_general(picks[h], c, (((0,), (0,)), ((), ())), preferred_element_type=f32)
-            residual = (dot(e[...], r) - base).astype(bf16)
-            res[h * rows : (h + 1) * rows, q * 2 * LANES : (q + 1) * 2 * LANES] = residual
-            coarse += dot(sends[h], residual)
-        for k in range(2):
-            out[2 * q + k, COARSE0:ROWS, :] = coarse[:, k * LANES : (k + 1) * LANES].astype(bf16)
-
-    word = lax.broadcasted_iota(jnp.int32, (K, rows), 0)
-    lane = lax.broadcasted_iota(jnp.int32, (rows, LANES), 1)
-    subs = M // 8
-
-    def book(x, carry):
-        total = jnp.zeros((K, LANES), f32)
-        for h, (_, p) in enumerate(halves):
-            first = pl.multiple_of((2 * x + core) * subs, subs)
-            codes = p[pl.ds(first, subs), :]
-            mine = res[h * rows : (h + 1) * rows, pl.ds(pl.multiple_of(x * LANES, LANES), LANES)]
-            for m in range(subs):
-                onehot = (word == codes[m : m + 1, :]).astype(bf16)
-                part = jnp.where(lane // (LANES // subs) == m, mine, jnp.zeros_like(mine))
-                total += dot(onehot, part)
-        out[x, BOOK0:COARSE0, :] = total.astype(bf16)
-        return carry
-
-    lax.fori_loop(0, X, book, 0)
+    def add(x, start, size, value):
+        both = sums[x, start : start + size, :] + value
+        out[x, BOOK0 + start : BOOK0 + start + size, :] = both.astype(bf16)
+
+    def codes_of(x):
+        return words[pl.ds(pl.multiple_of(x * SUBS, SUBS), SUBS), :]
+
+    assigned = words[X * SUBS : X * SUBS + 1, :]
+    residual_sums(e1, rot, cent, assigned, codes_of, res, add)
 
 
 def first_sums(arrived, out):
@@ -162,19 +208,39 @@
     vectors = rows * lax.axis_size(DP_SUB)
     core = lax.axis_index("c").reshape(1)
     place = lax.axis_index("zs").reshape(1)
-    words = jnp.concatenate([codes.T, jnp.broadcast_to(assignments[None, :], (8, rows))], axis=0)
     swap = [(0, 1), (1, 0)]
     other = lax.ppermute(embeddings, "c", swap)
-    other_words = lax.ppermute(words, "c", swap)
+    half = X * LANES
+    sums, words, mine, rotation, centroids = pl.pallas_call(
+        own_sums,
+        out_shape=(
+            jax.ShapeDtypeStruct((X, K + CENTS, LANES), f32),
+            jax.ShapeDtypeStruct(((X + 1) * SUBS, rows), jnp.int32),
+            jax.ShapeDtypeStruct((rows, D), bf16),
+            jax.ShapeDtypeStruct((D, half), bf16),
+            jax.ShapeDtypeStruct((CENTS, half), bf16),
+        ),
+        in_specs=[SMEM] * 2 + [HBM] * 5,
+        out_specs=(VMEM,) * 5,
+        scratch_shapes=[
+            pltpu.VMEM((M, rows), jnp.int32),
+            pltpu.VMEM((rows,), jnp.int32),
+            pltpu.VMEM((rows, half), bf16),
+            pltpu.SemaphoreType.DMA((3 + 2 * X,)),
+        ],
+        compiler_params=params(24),
+        name="own_sums",
+    )(core, place, *(pltpu.with_memory_space_constraint(v, pltpu.HBM) for v in (embeddings, rotation, centroids, codes.T, assignments)))
+    words = lax.ppermute(words, "c", swap)
     parts = pl.pallas_call(
         partial_sums,
         out_shape=jax.ShapeDtypeStruct((X, ROWS, LANES), bf16),
-        in_specs=[SMEM] * 2 + [VMEM] * 6,
+        in_specs=[SMEM] + [VMEM] * 6,
         out_specs=VMEM,
-        scratch_shapes=[pltpu.VMEM((D // 2, 2 * rows), bf16), pltpu.VMEM((2 * rows, D // 2), bf16)],
-        compiler_params=params(32),
+        scratch_shapes=[pltpu.VMEM((half, 2 * rows), bf16), pltpu.VMEM((rows, half), bf16)],
+        compiler_params=params(24),
         name="partial_sums",
-    )(core, place, embeddings, other, rotation, centroids, words, other_words)
+    )(core, mine, other, rotation, centroids, words, sums)
     arrived = lax.all_to_all(parts, "x", split_axis=0, concat_axis=0, tiled=True)
     pieces = pl.pallas_call(
         first_sums,

time: 107 us -> 105 us (0.981)
  local copies, waits for them, and re-layouts: 4.48 us -> 0.05 us
  Pallas kernels: 10.1 us -> 13.9 us
    pallas_call x0 -> x1, Pallas kernels: none -> 6.3 us  [per_device(): pl.pallas_call(own_sums, out_shape=(jax.ShapeDtypeStruct((X, K + CENTS, L...]
    unnamed x6 -> x0, local copies, waits for them, and re-layouts: 3.74 us -> none
    pallas_call x1, Pallas kernels: 8.45 us -> 5.88 us  [per_device(): pl.pallas_call(partial_sums, out_shape=jax.ShapeDtypeStruct((X, ROWS, LAN...]
  transfers between devices with their start and end apart: 2 -> 2, of which waited for: 1 -> 1; matrix products, arithmetic and copies ran while one was open for 2% -> 0% of each run, Pallas kernels for 0% -> 6%
where the time goes in v3:
time: 105 us
  blocking collectives  84.8 us (81%)
  Pallas kernels  13.9 us (13%)
  starting transfers between devices  4.33 us (4%)
    all_to_all x1, blocking collectives, per_device(): lax.all_to_all(parts, 'x', split_axis=0, concat_axis=0, tiled=True)  23.6 us
    all_to_all x1, blocking collectives, per_device(): lax.all_to_all(pieces, 'zs', split_axis=0, concat_axis=0, tiled=True)  23.3 us
    all_to_all x1, blocking collectives, per_device(): lax.all_to_all(pieces, OWNERS, split_axis=0, concat_axis=0, tiled=True)  23 us
    all_to_all x1, blocking collectives, per_device(): lax.all_to_all(spread, OWNERS, split_axis=0, concat_axis=0, tiled=True)  14.9 us
    pallas_call x1, Pallas kernels, per_device(): pl.pallas_call(own_sums, out_shape=(jax.ShapeDtypeStruct((X, K + CENTS, L...  6.3 us
    pallas_call x1, Pallas kernels, per_device(): pl.pallas_call(partial_sums, out_shape=jax.ShapeDtypeStruct((X, ROWS, LAN...  5.88 us
    ppermute x1, starting transfers between devices, per_device(): words = lax.ppermute(words, 'c', swap)  2.41 us
  transfers between devices with their start and end apart: 2, of which 1 were waited for; matrix products, arithmetic and copies ran while one was open for 0% of the time, Pallas kernels for 6%

profile of v3, /device:TPU:8, one launch (start us, length us, event | category | flops | bytes accessed | tf_op | source)
XLA Modules:
  0.0 104.7 jit_solution(9930956833464146005)
XLA Ops:
  0.6 1.9 %collective-permute-start = (bf16[512,1024]{1,0:T(8,128)(2,1)}, bf16[512,1024]{1,0:T(8,128)(2,1)S(1)}, u32[]{:S(2)}, u32[]{:S(2)}) collective-permute-start(bf16[512,1024]{1,0:T(8,128)(2,1)} %e_in.1), channel_id=1, source_target_pairs={{0,1},{1,0},{2,3},{3,2},{4,5},{5,4},{6,7},{7,6},{8,9},{9,8},{10,11... | collective-permute-start | bytes 3145736 | tf_op jit(solution)/shard_map/ppermute | solution.py:212
  2.6 6.3 %own_sums.1 = (f32[4,352,128]{2,1,0:T(8,128)S(1)}, s32[40,512]{1,0:T(8,128)S(1)}, bf16[512,1024]{1,0:T(8,128)(2,1)S(1)}, bf16[1024,512]{1,0:T(8,128)(2,1)S(1)}, bf16[96,512]{1,0:T(8,128)(2,1)S(1)}) custom-call(s32[1]{0:T(128)} %bitcast.1.core_ref, s32[1]{0:T(128)} %bitcast.place_ref.refs_0_, bf16[512,1024]{1,0:T(8,128)(2,1)} %e_in.1, ...), custom_call_target="tpu_custom_call" | custom-call | tf_op jit(solution)/shard_map/own_sums/pallas_call | solution.py:214
  8.9 2.4 %collective-permute-start.1 = (s32[40,512]{1,0:T(8,128)S(1)}, s32[40,512]{1,0:T(8,128)S(1)}, u32[]{:S(2)}, u32[]{:S(2)}) collective-permute-start(s32[40,512]{1,0:T(8,128)S(1)} %get-tuple-element.15), channel_id=1, source_target_pairs={{0,1},{1,0},{2,3},{3,2},{4,5},{5,4},{6,7},{7,6},{8,9},{9,8},{10,11... | collective-permute-start | bytes 245768 | tf_op jit(solution)/shard_map/ppermute | solution.py:234
  11.3 0.9 collective-permute-done.1.words
  12.2 0.0 collective-permute-done.e1
  12.2 5.9 %partial_sums.1 = bf16[4,1376,128]{2,1,0:T(8,128)(2,1)S(1)} custom-call(s32[1]{0:T(128)} %bitcast.1.core_ref, bf16[512,1024]{1,0:T(8,128)(2,1)S(1)} %get-tuple-element.12.e0, bf16[512,1024]{1,0:T(8,128)(2,1)S(1)} %collective-permute-done.e1, bf16[1024,512]{1,0:T(8,128)(2,1)S(1)} %get-tuple-element.13.rot, bf16[96,512]{1,0:T(8,128)(2,1)S(1)} %get-tuple-element.14.cent, ...), custom_call_target="tpu_custom_call" | custom-call | tf_op jit(solution)/shard_map/partial_sums/pallas_call | solution.py:235
  18.1 23.6 %all_to_all.20.arrived = bf16[4,1376,128]{2,1,0:T(8,128)(2,1)S(1)} all-to-all(bf16[4,1376,128]{2,1,0:T(8,128)(2,1)S(1)} %partial_sums.1), channel_id=1, replica_groups=mesh['zs'=6,'zf'=2,'y'=8,'x'=4,'c'=2] {'x'}, dimensions={0} | all-to-all | bytes 2818048 | tf_op jit(solution)/shard_map/all_to_all | solution.py:244
  41.7 0.2 first_sums.1
  41.8 23.0 %all_to_all.21.arrived = bf16[16,96,128]{2,1,0:T(8,128)(2,1)S(1)} all-to-all(bf16[16,96,128]{2,1,0:T(8,128)(2,1)S(1)} %first_sums.1), channel_id=1, replica_groups=mesh['zs'=6,'zf'=2,'y'=8,'x'=4,'c'=2] {'zf','y'}, dimensions={0} | all-to-all | bytes 786432 | tf_op jit(solution)/shard_map/all_to_all | solution.py:253
  64.9 0.1 second_sums.1
  64.9 23.3 %all_to_all.22.refs_1_ = bf16[6,112,128]{2,1,0:T(8,128)(2,1)S(1)} all-to-all(bf16[6,112,128]{2,1,0:T(8,128)(2,1)S(1)} %second_sums.1), channel_id=1, replica_groups=mesh['zs'=6,'zf'=2,'y'=8,'x'=4,'c'=2] {'zs'}, dimensions={0} | all-to-all | bytes 344064 | tf_op jit(solution)/shard_map/all_to_all | solution.py:262
  88.2 0.5 owned_sums.1
  88.8 0.1 broadcast_in_dim.2
  88.8 14.9 %all_to_all.23 = f16[16,88,128]{2,1,0:T(8,128)(2,1)S(1)} all-to-all(f16[16,88,128]{2,1,0:T(8,128)(2,1)S(1)} %broadcast_in_dim.2), channel_id=1, replica_groups=mesh['zs'=6,'zf'=2,'y'=8,'x'=4,'c'=2] {'zf','y'}, dimensions={0} | all-to-all | bytes 720896 | tf_op jit(solution)/shard_map/all_to_all | solution.py:275
  103.8 0.9 laid_out.1
  (2 shorter events, 0.1 us)
Async XLA Ops:
  0.6 11.6 %collective-permute-start = (bf16[512,1024]{1,0:T(8,128)(2,1)}, bf16[512,1024]{1,0:T(8,128)(2,1)S(1)}, u32[]{:S(2)}, u32[]{:S(2)}) collective-permute-start(bf16[512,1024]{1,0:T(8,128)(2,1)} %e_in.1), channel_id=1, source_target_pairs={{0,1},{1,0},{2,3},{3,2},{4,5},{5,4},{6,7},{7,6},{8,9},{9,8},{10,11... | collective-permute-start | bytes 3145736 | tf_op jit(solution)/shard_map/ppermute | solution.py:212
  8.9 3.3 %collective-permute-start.1 = (s32[40,512]{1,0:T(8,128)S(1)}, s32[40,512]{1,0:T(8,128)S(1)}, u32[]{:S(2)}, u32[]{:S(2)}) collective-permute-start(s32[40,512]{1,0:T(8,128)S(1)} %get-tuple-element.15), channel_id=1, source_target_pairs={{0,1},{1,0},{2,3},{3,2},{4,5},{5,4},{6,7},{7,6},{8,9},{9,8},{10,11... | collective-permute-start | bytes 245768 | tf_op jit(solution)/shard_map/ppermute | solution.py:234

commit v4 on v2

v4 whole, which is shorter than its diff:
```python
import jax
import jax.numpy as jnp
from jax import lax
from jax.experimental import pallas as pl
from jax.experimental.pallas import tpu as pltpu
from jax.sharding import Mesh
from jax.sharding import PartitionSpec as P

D = 1024
M = 64
K = 256
CENTS = 96
LANES = 128
SUBS = 8
X = 4
YS = 4
YF = 2
ZF = 2
ZS = 6
NEAR = ("zf",)
FAR = ("yf", "ys")
PARTS = 2
OWNERS = NEAR + FAR
PEERS = ZF * YF * YS
DP = ("zs", "zf", "ys", "yf")
DP_SUB = ("zs", "zf", "ys", "yf", "x", "c")
BOOK0 = D
COARSE0 = D + K
ROWS = D + K + CENTS
GP = D // PEERS
BP = K // PEERS
CP = CENTS // PEERS
C0 = GP + BP
PART = C0 + 16
ONE = PART + BP
SPREAD = C0 + 8
bf16 = jnp.bfloat16
f16 = jnp.float16
f32 = jnp.float32
VMEM = pl.BlockSpec(memory_space=pltpu.VMEM)
SMEM = pl.BlockSpec(memory_space=pltpu.SMEM)
HBM = pl.BlockSpec(memory_space=pltpu.HBM)


def params(mib):
    return pltpu.CompilerParams(vmem_limit_bytes=mib * 2**20)


def dot(a, b):
    return jnp.dot(a, b, preferred_element_type=f32)


def columns(core, x):
    return pl.ds(pl.multiple_of((2 * x + core) * LANES, LANES), LANES)


def residual_sums(e, rot, cent, assigned, codes, res):
    rows = e.shape[0]
    label = lax.broadcasted_iota(jnp.int32, (CENTS, rows), 0)
    owner = label // CP
    zf, yf, ys = owner // (YF * YS), owner // YS % YF, owner % YS
    sent = (((label % CP) * ZF + zf) * YS + ys) * YF + yf
    pick = (label == assigned).astype(bf16)
    send = (sent == assigned).astype(bf16)
    coarse = []
    for q in range(X // 2):
        pair = slice(q * 2 * LANES, (q + 1) * 2 * LANES)
        base = lax.dot_general(
            pick, cent[:, pair], (((0,), (0,)), ((), ())), preferred_element_type=f32
        )
        residual = (dot(e[...], rot[:, pair]) - base).astype(bf16)
        res[:, pair] = residual
        coarse.append(dot(send, residual))
    return coarse


def book_sums(res, codes):
    rows = res.shape[0]
    word = lax.broadcasted_iota(jnp.int32, (K, rows), 0)
    lane = lax.broadcasted_iota(jnp.int32, (rows, LANES), 1)
    total = jnp.zeros((K, LANES), f32)
    for m in range(SUBS):
        onehot = (word == codes[m : m + 1, :]).astype(bf16)
        part = jnp.where(lane // (LANES // SUBS) == m, res, jnp.zeros_like(res))
        total += dot(onehot, part)
    return total


def other_words(core_ref, place_ref, codes_in, assigned_in, words, assigned, sems):
    core = core_ref[0]
    copies = [pltpu.make_async_copy(assigned_in, assigned, sems.at[X])]
    for x in range(X):
        theirs = pl.ds(pl.multiple_of((2 * x + 1 - core) * SUBS, SUBS), SUBS)
        copies.append(
            pltpu.make_async_copy(
                codes_in.at[theirs, :], words.at[x * SUBS : (x + 1) * SUBS, :], sems.at[x]
            )
        )
    for copy in copies:
        copy.start()
    for copy in copies:
        copy.wait()
    words[X * SUBS :, :] = jnp.broadcast_to(assigned[...].reshape(1, -1), (SUBS, words.shape[1]))


def partial_sums(
    core_ref, e_in, rot_in, cent_in, codes_in, assigned_in, e1, words,
    out, e0, rot, cent, codes, assigned_ref, turned, res, sems,
):
    core = core_ref[0]
    rows = e1.shape[0]
    first = pltpu.make_async_copy(e_in, e0, sems.at[0])
    first.start()
    copies = [pltpu.make_async_copy(assigned_in, assigned_ref, sems.at[1])]
    for x in range(X):
        here = slice(x * LANES, (x + 1) * LANES)
        lanes = columns(core, x)
        mine = pl.ds(pl.multiple_of((2 * x + core) * SUBS, SUBS), SUBS)
        copies += [
            pltpu.make_async_copy(rot_in.at[:, lanes], rot.at[:, here], sems.at[2 + 3 * x]),
            pltpu.make_async_copy(cent_in.at[:, lanes], cent.at[:, here], sems.at[3 + 3 * x]),
            pltpu.make_async_copy(
                codes_in.at[mine, :], codes.at[x * SUBS : (x + 1) * SUBS, :], sems.at[4 + 3 * x]
            ),
        ]
    for copy in copies:
        copy.start()
    for x in range(X):
        turned[x * LANES : (x + 1) * LANES, rows:] = e1[:, columns(core, x)].T
    first.wait()
    for x in range(X):
        turned[x * LANES : (x + 1) * LANES, :rows] = e0[:, columns(core, x)].T
    wide = 256
    grams = D // PARTS
    for n in range(D // wide):
        cols = slice(n * wide, (n + 1) * wide)
        g = dot(turned[:, :rows], e0[:, cols]) + dot(turned[:, rows:], e1[:, cols])
        for x in range(X):
            for k in range(wide // LANES):
                part, row = divmod((n * (wide // LANES) + k) * LANES, grams)
                out[part, x, row : row + LANES, :] = g[
                    x * LANES : (x + 1) * LANES, k * LANES : (k + 1) * LANES
                ].astype(bf16)
    for copy in copies:
        copy.wait()
    own = residual_sums(e0, rot, cent, assigned_ref[...].reshape(1, -1), codes, res.at[:rows])
    theirs = residual_sums(e1, rot, cent, words[X * SUBS : X * SUBS + 1, :], words, res.at[rows:])
    books, cents = K // PARTS, CENTS // PARTS
    book0, coarse0 = grams, grams + books
    for q in range(X // 2):
        coarse = (own[q] + theirs[q]).astype(bf16)
        for k in range(2):
            for part in range(PARTS):
                piece = coarse[part * cents : (part + 1) * cents, k * LANES : (k + 1) * LANES]
                out[part, 2 * q + k, coarse0:, :] = piece

    for x in range(X):
        subs = slice(x * SUBS, (x + 1) * SUBS)
        lanes = slice(x * LANES, (x + 1) * LANES)
        total = book_sums(res[:rows, lanes], codes[subs, :])
        total = (total + book_sums(res[rows:, lanes], words[subs, :])).astype(bf16)
        for part in range(PARTS):
            out[part, x, book0:coarse0, :] = total[part * books : (part + 1) * books]
def first_sums(arrived, out):
    def summed(a, b):
        return arrived[:, a:b, :].astype(f32).sum(axis=0)

    grams, books = D // PARTS, K // PARTS
    coarse = summed(grams + books, ROWS // PARTS)
    zeros = jnp.zeros((PART - C0 - CP, LANES), f32)
    for q in range(out.shape[0]):
        out[q, :GP, :] = summed(q * GP, (q + 1) * GP).astype(bf16)
        out[q, GP:C0, :] = summed(grams + q * BP, grams + (q + 1) * BP).astype(bf16)
        mine = coarse[q * CP : (q + 1) * CP, :]
        out[q, C0:PART, :] = jnp.concatenate([mine, zeros], axis=0).astype(bf16)


def second_sums(arrived, out):
    total = arrived[...].astype(f32).sum(axis=0)
    high = total.astype(bf16)
    low = total - high.astype(f32)
    coarse = jnp.concatenate([total[C0 : C0 + 8], low[C0 : C0 + 8]], axis=0).astype(bf16)
    book = low[GP:C0].astype(bf16)
    for i in range(out.shape[0]):
        out[i, :C0, :] = high[:C0]
        out[i, C0:PART, :] = coarse
        out[i, PART:ONE, :] = book


def owned_sums(place_ref, arrived, coarse_out, mine, *, vectors):
    total = arrived[...].astype(f32).sum(axis=0)
    coarse = total[C0 : C0 + 8] + total[C0 + 8 : C0 + 16]
    row = lax.broadcasted_iota(jnp.int32, (8, LANES), 0)
    own = jnp.where(row == place_ref[0], coarse, 0.0).sum(axis=0, keepdims=True)
    coarse_out[...] = own * (CENTS / vectors) ** 0.5
    gram = total[:GP] * (1.0 / vectors)
    book = (total[GP:C0] + total[PART:ONE]) * (K / vectors) ** 0.5

    def scaled(v):
        top = jnp.max(jnp.abs(v), keepdims=True)
        power = jnp.ceil(jnp.log2(jnp.maximum(top, 2.0**-100)))
        return v * jnp.exp2(-power), jnp.broadcast_to(power, (8, LANES))

    gram, gram_power = scaled(gram)
    book, book_power = scaled(book)
    mine[:GP, :] = gram
    mine[GP:C0, :] = book
    mine[C0:SPREAD, :] = jnp.where(row == 0, gram_power, book_power)


def laid_out(arrived, gram, book):
    for q in range(PEERS):
        power = jnp.exp2(arrived[q, C0:SPREAD, :])
        j, top = q * GP // LANES, q * GP % LANES
        gram[top : top + GP, j * LANES : (j + 1) * LANES] = arrived[q, :GP, :] * power[0:1]
        book[q * BP : (q + 1) * BP, :] = arrived[q, GP:C0, :] * power[1:2]


def per_device(embeddings, rotation, centroids, assignments, codes):
    rows = embeddings.shape[0]
    vectors = rows * lax.axis_size(DP_SUB)
    core = lax.axis_index("c").reshape(1)
    place = lax.axis_index("zs").reshape(1)
    swap = [(0, 1), (1, 0)]
    other = lax.ppermute(embeddings, "c", swap)
    half = X * LANES
    inputs = (embeddings, rotation, centroids, codes.T, assignments)
    inputs = tuple(pltpu.with_memory_space_constraint(v, pltpu.HBM) for v in inputs)
    words = pl.pallas_call(
        other_words,
        out_shape=jax.ShapeDtypeStruct(((X + 1) * SUBS, rows), jnp.int32),
        in_specs=[SMEM] * 2 + [HBM] * 2,
        out_specs=VMEM,
        scratch_shapes=[pltpu.VMEM((rows,), jnp.int32), pltpu.SemaphoreType.DMA((X + 1,))],
        compiler_params=params(16),
        name="other_words",
    )(core, place, *inputs[3:])
    words = lax.ppermute(words, "c", swap)
    parts = pl.pallas_call(
        partial_sums,
        out_shape=jax.ShapeDtypeStruct((PARTS, X, ROWS // PARTS, LANES), bf16),
        in_specs=[SMEM] + [HBM] * 5 + [VMEM] * 2,
        out_specs=VMEM,
        scratch_shapes=[
            pltpu.VMEM((rows, D), bf16),
            pltpu.VMEM((D, half), bf16),
            pltpu.VMEM((CENTS, half), bf16),
            pltpu.VMEM((X * SUBS, rows), jnp.int32),
            pltpu.VMEM((rows,), jnp.int32),
            pltpu.VMEM((half, 2 * rows), bf16),
            pltpu.VMEM((2 * rows, half), bf16),
            pltpu.SemaphoreType.DMA((2 + 3 * X,)),
        ],
        compiler_params=params(32),
        name="partial_sums",
    )(core, *inputs, other, words)
    parts = parts.reshape(PARTS * X, ROWS // PARTS, LANES)
    arrived = lax.all_to_all(parts, NEAR + ("x",), split_axis=0, concat_axis=0, tiled=True)
    pieces = pl.pallas_call(
        first_sums,
        out_shape=jax.ShapeDtypeStruct((PEERS // PARTS, PART, LANES), bf16),
        in_specs=[VMEM],
        out_specs=VMEM,
        compiler_params=params(16),
        name="first_sums",
    )(arrived)
    arrived = lax.all_to_all(pieces, FAR, split_axis=0, concat_axis=0, tiled=True)
    pieces = pl.pallas_call(
        second_sums,
        out_shape=jax.ShapeDtypeStruct((ZS, ONE, LANES), bf16),
        in_specs=[VMEM],
        out_specs=VMEM,
        compiler_params=params(16),
        name="second_sums",
    )(arrived)
    arrived = lax.all_to_all(pieces, "zs", split_axis=0, concat_axis=0, tiled=True)
    coarse_sums, mine = pl.pallas_call(
        lambda *refs: owned_sums(*refs, vectors=vectors),
        out_shape=(
            jax.ShapeDtypeStruct((1, LANES), f32),
            jax.ShapeDtypeStruct((SPREAD, LANES), f32),
        ),
        in_specs=[SMEM, VMEM],
        out_specs=(VMEM, VMEM),
        compiler_params=params(16),
        name="owned_sums",
    )(place, arrived)
    spread = jnp.broadcast_to(mine.astype(f16)[None], (PEERS, SPREAD, LANES))
    arrived = lax.all_to_all(spread, OWNERS, split_axis=0, concat_axis=0, tiled=True)
    gram, codebook_sums = pl.pallas_call(
        laid_out,
        out_shape=(jax.ShapeDtypeStruct((LANES, D), f32), jax.ShapeDtypeStruct((K, LANES), f32)),
        in_specs=[VMEM],
        out_specs=(VMEM, VMEM),
        compiler_params=params(16),
        name="laid_out",
    )(arrived.astype(f32))
    return gram, coarse_sums, codebook_sums


def solution(mesh):
    finer = Mesh(mesh.devices.reshape(ZS, ZF, YS, YF, X, 2), DP_SUB)
    return jax.shard_map(
        per_device,
        mesh=finer,
        in_specs=(P(DP_SUB, None), P(), P(), P(DP_SUB), P(DP_SUB, None)),
        out_specs=(P(("x", "c"), None), P(DP, ("x", "c")), P(None, ("x", "c"))),
        check_vma=False,
    )
```

time: 107 us -> 99 us (0.925)
  blocking collectives: 84.8 us -> 80.3 us
  local copies, waits for them, and re-layouts: 4.48 us -> 0.05 us
  Pallas kernels: 10.1 us -> 12.3 us
    unnamed x6 -> x0, local copies, waits for them, and re-layouts: 3.74 us -> none
    all_to_all x2, blocking collectives: 46.6 us -> 43.1 us  [the longest x1 26 us: per_device(): lax.all_to_all(parts, NEAR + ('x',), split_axis=0, concat_axis=0, tiled=T...]
    pallas_call x2 -> x3, Pallas kernels: 8.63 us -> 10.8 us  [the longest x1 9.78 us: per_device(): pl.pallas_call(partial_sums, out_shape=jax.ShapeDtypeStruct((PARTS, X, RO...]
    all_to_all x1, blocking collectives: 14.9 us -> 13.7 us  [per_device(): lax.all_to_all(spread, OWNERS, split_axis=0, concat_axis=0, tiled=True)]
  transfers between devices with their start and end apart: 2 -> 2, of which waited for: 1 -> 1; matrix products, arithmetic and copies ran while one was open for 2% -> 0% of each run, Pallas kernels for 0% -> 1%
where the time goes in v4:
time: 99 us; the launch traced here: 98.6 us
  blocking collectives  80.3 us (81%)
  Pallas kernels  12.3 us (12%)
  starting transfers between devices  4.33 us (4%)
    all_to_all x1, blocking collectives, per_device(): lax.all_to_all(parts, NEAR + ('x',), split_axis=0, concat_axis=0, tiled=T...  26 us
    all_to_all x1, blocking collectives, per_device(): lax.all_to_all(pieces, 'zs', split_axis=0, concat_axis=0, tiled=True)  23.6 us
    all_to_all x1, blocking collectives, per_device(): lax.all_to_all(pieces, FAR, split_axis=0, concat_axis=0, tiled=True)  17.1 us
    all_to_all x1, blocking collectives, per_device(): lax.all_to_all(spread, OWNERS, split_axis=0, concat_axis=0, tiled=True)  13.7 us
    pallas_call x1, Pallas kernels, per_device(): pl.pallas_call(partial_sums, out_shape=jax.ShapeDtypeStruct((PARTS, X, RO...  9.78 us
    ppermute x1, starting transfers between devices, per_device(): words = lax.ppermute(words, 'c', swap)  2.41 us
  transfers between devices with their start and end apart: 2, of which 1 were waited for; matrix products, arithmetic and copies ran while one was open for 0% of the time, Pallas kernels for 1%

profile of v4, /device:TPU:8, one launch (start us, length us, event | category | flops | bytes accessed | tf_op | source)
XLA Modules:
  0.0 98.6 jit_solution(7022485879825015520)
XLA Ops:
  0.6 1.9 %collective-permute-start = (bf16[512,1024]{1,0:T(8,128)(2,1)}, bf16[512,1024]{1,0:T(8,128)(2,1)S(1)}, u32[]{:S(2)}, u32[]{:S(2)}) collective-permute-start(bf16[512,1024]{1,0:T(8,128)(2,1)} %e_in.1), channel_id=1, source_target_pairs={{0,1},{1,0},{2,3},{3,2},{4,5},{5,4},{6,7},{7,6},{8,9},{9,8},{10,11... | collective-permute-start | bytes 3145736 | tf_op jit(solution)/shard_map/ppermute | solution.py:225
  2.6 0.8 other_words.1
  3.4 2.4 %collective-permute-start.1 = (s32[40,512]{1,0:T(8,128)S(1)}, s32[40,512]{1,0:T(8,128)S(1)}, u32[]{:S(2)}, u32[]{:S(2)}) collective-permute-start(s32[40,512]{1,0:T(8,128)S(1)} %other_words.1), channel_id=1, source_target_pairs={{0,1},{1,0},{2,3},{3,2},{4,5},{5,4},{6,7},{7,6},{8,9},{9,8},{10,11... | collective-permute-start | bytes 245768 | tf_op jit(solution)/shard_map/ppermute | solution.py:238
  5.8 0.9 collective-permute-done.1.words
  6.7 0.0 collective-permute-done.e1
  6.7 9.8 %partial_sums.1 = bf16[2,4,688,128]{3,2,1,0:T(8,128)(2,1)S(1)} custom-call(s32[1]{0:T(128)} %bitcast.1.core_ref, bf16[512,1024]{1,0:T(8,128)(2,1)} %e_in.1, bf16[1024,1024]{1,0:T(8,128)(2,1)} %rot_in.1, bf16[96,1024]{1,0:T(8,128)(2,1)} %cent_in.1, s32[64,512]{1,0:T(8,128)} %bitcast.6, s32[512]{0:T(512)} %assigned_in.3, ...), custom_call_target="tpu_custom_call" | custom-call | tf_op jit(solution)/shard_map/partial_sums/pallas_call | solution.py:239
  16.5 26.0 %all_to_all.20.arrived = bf16[8,688,128]{2,1,0:T(8,128)(2,1)S(1)} all-to-all(bf16[8,688,128]{2,1,0:T(8,128)(2,1)S(1)} %bitcast.4), channel_id=1, replica_groups=mesh['zs'=6,'zf'=2,'ys'=4,'yf'=2,'x'=4,'c'=2] {'zf','x'}, dimensions={0} | all-to-all | bytes 2818048 | tf_op jit(solution)/shard_map/all_to_all | solution.py:258
  42.5 0.2 first_sums.1
  42.7 17.1 %all_to_all.21.arrived = bf16[8,96,128]{2,1,0:T(8,128)(2,1)S(1)} all-to-all(bf16[8,96,128]{2,1,0:T(8,128)(2,1)S(1)} %first_sums.1), channel_id=1, replica_groups=mesh['zs'=6,'zf'=2,'ys'=4,'yf'=2,'x'=4,'c'=2] {'yf','ys'}, dimensions={0} | all-to-all | bytes 393216 | tf_op jit(solution)/shard_map/all_to_all | solution.py:267
  59.8 23.6 %all_to_all.22.refs_1_ = bf16[6,112,128]{2,1,0:T(8,128)(2,1)S(1)} all-to-all(bf16[6,112,128]{2,1,0:T(8,128)(2,1)S(1)} %second_sums.1), channel_id=1, replica_groups=mesh['zs'=6,'zf'=2,'ys'=4,'yf'=2,'x'=4,'c'=2] {'zs'}, dimensions={0} | all-to-all | bytes 344064 | tf_op jit(solution)/shard_map/all_to_all | solution.py:276
  83.4 0.5 owned_sums.1
  84.0 0.1 broadcast_in_dim.2
  84.0 13.7 %all_to_all.23 = f16[16,88,128]{2,1,0:T(8,128)(2,1)S(1)} all-to-all(f16[16,88,128]{2,1,0:T(8,128)(2,1)S(1)} %broadcast_in_dim.2), channel_id=1, replica_groups=mesh['zs'=6,'zf'=2,'ys'=4,'yf'=2,'x'=4,'c'=2] {'zf','yf','ys'}, dimensions={0} | all-to-all | bytes 720896 | tf_op jit(solution)/shard_map/all_to_all | solution.py:289
  97.7 0.9 laid_out.1
  (3 shorter events, 0.1 us)
Async XLA Ops:
  0.6 6.1 %collective-permute-start = (bf16[512,1024]{1,0:T(8,128)(2,1)}, bf16[512,1024]{1,0:T(8,128)(2,1)S(1)}, u32[]{:S(2)}, u32[]{:S(2)}) collective-permute-start(bf16[512,1024]{1,0:T(8,128)(2,1)} %e_in.1), channel_id=1, source_target_pairs={{0,1},{1,0},{2,3},{3,2},{4,5},{5,4},{6,7},{7,6},{8,9},{9,8},{10,11... | collective-permute-start | bytes 3145736 | tf_op jit(solution)/shard_map/ppermute | solution.py:225
  3.4 3.3 %collective-permute-start.1 = (s32[40,512]{1,0:T(8,128)S(1)}, s32[40,512]{1,0:T(8,128)S(1)}, u32[]{:S(2)}, u32[]{:S(2)}) collective-permute-start(s32[40,512]{1,0:T(8,128)S(1)} %other_words.1), channel_id=1, source_target_pairs={{0,1},{1,0},{2,3},{3,2},{4,5},{5,4},{6,7},{7,6},{8,9},{9,8},{10,11... | collective-permute-start | bytes 245768 | tf_op jit(solution)/shard_map/ppermute | solution.py:238

commit v5 on v2

v5 whole, which is shorter than its diff:
```python
import jax
import jax.numpy as jnp
from jax import lax
from jax.experimental import pallas as pl
from jax.experimental.pallas import tpu as pltpu
from jax.sharding import Mesh
from jax.sharding import PartitionSpec as P

D = 1024
M = 64
K = 256
CENTS = 96
LANES = 128
SUBS = 8
X = 4
YS = 4
YF = 2
ZF = 2
ZS = 6
NEAR = ("zf",)
FAR = ("yf", "ys")
PARTS = 2
OWNERS = NEAR + FAR
PEERS = ZF * YF * YS
DP = ("zs", "zf", "ys", "yf")
DP_SUB = ("zs", "zf", "ys", "yf", "x", "c")
BOOK0 = D
COARSE0 = D + K
ROWS = D + K + CENTS
GP = D // PEERS
BP = K // PEERS
CP = CENTS // PEERS
C0 = GP + BP
PART = C0 + 16
ONE = PART + BP
SPREAD = C0 + 8
bf16 = jnp.bfloat16
f16 = jnp.float16
f32 = jnp.float32
VMEM = pl.BlockSpec(memory_space=pltpu.VMEM)
SMEM = pl.BlockSpec(memory_space=pltpu.SMEM)
HBM = pl.BlockSpec(memory_space=pltpu.HBM)


def params(mib):
    return pltpu.CompilerParams(vmem_limit_bytes=mib * 2**20)


def dot(a, b):
    return jnp.dot(a, b, preferred_element_type=f32)


def columns(core, x):
    return pl.ds(pl.multiple_of((2 * x + core) * LANES, LANES), LANES)


def book_sums(res, codes):
    rows = res.shape[0]
    word = lax.broadcasted_iota(jnp.int32, (K, rows), 0)
    lane = lax.broadcasted_iota(jnp.int32, (rows, LANES), 1)
    total = jnp.zeros((K, LANES), f32)
    for m in range(SUBS):
        onehot = (word == codes[m : m + 1, :]).astype(bf16)
        part = jnp.where(lane // (LANES // SUBS) == m, res, jnp.zeros_like(res))
        total += dot(onehot, part)
    return total


def half_sums(whose, e, rot, cent, codes, assigned, out, turned, wait=None):
    rows = e.shape[0]
    for x in range(X):
        turned[x * LANES : (x + 1) * LANES, :] = e[:, columns(whose, x)].T
    wide = 256
    grams, books, cents = D // PARTS, K // PARTS, CENTS // PARTS
    book0, coarse0 = grams, grams + books
    for n in range(D // wide):
        g = dot(turned[...], e[:, n * wide : (n + 1) * wide])
        for x in range(X):
            for k in range(wide // LANES):
                part, row = divmod((n * (wide // LANES) + k) * LANES, grams)
                out[part, x, row : row + LANES, :] = g[
                    x * LANES : (x + 1) * LANES, k * LANES : (k + 1) * LANES
                ].astype(out.dtype)
    if wait is not None:
        wait()
    label = lax.broadcasted_iota(jnp.int32, (CENTS, rows), 0)
    owner = label // CP
    zf, yf, ys = owner // (YF * YS), owner // YS % YF, owner % YS
    sent = (((label % CP) * ZF + zf) * YS + ys) * YF + yf
    named = assigned[...].reshape(1, rows)
    pick = (label == named).astype(bf16)
    send = (sent == named).astype(bf16)
    for q in range(X // 2):
        pair = (columns(whose, 2 * q), columns(whose, 2 * q + 1))
        c = jnp.concatenate([cent[:, p] for p in pair], axis=1)
        r = jnp.concatenate([rot[:, p] for p in pair], axis=1)
        base = lax.dot_general(pick, c, (((0,), (0,)), ((), ())), preferred_element_type=f32)
        residual = (dot(e[...], r) - base).astype(bf16)
        coarse = dot(send, residual).astype(out.dtype)
        for k in range(2):
            x = 2 * q + k
            lanes = slice(k * LANES, (k + 1) * LANES)
            subs = pl.ds(pl.multiple_of((2 * x + whose) * SUBS, SUBS), SUBS)
            total = book_sums(residual[:, lanes], codes[subs, :]).astype(out.dtype)
            for part in range(PARTS):
                out[part, x, book0:coarse0, :] = total[part * books : (part + 1) * books]
                out[part, x, coarse0:, :] = coarse[part * cents : (part + 1) * cents, lanes]


def sibling_sums(
    core_ref, place_ref, e_in, rot_in, cent_in, codes_in, assigned_in,
    out, e, rot, cent, codes, assigned, turned, sems,
):
    pairs = (
        (e_in, e), (assigned_in, assigned), (cent_in, cent), (codes_in, codes), (rot_in, rot),
    )
    copies = [pltpu.make_async_copy(a, b, sems.at[i]) for i, (a, b) in enumerate(pairs)]
    for copy in copies:
        copy.start()
    copies[0].wait()

    def wait():
        for copy in copies[1:]:
            copy.wait()

    half_sums(1 - core_ref[0], e, rot, cent, codes, assigned, out, turned, wait)


def own_sums(core_ref, e, rot, cent, codes, assigned, out, turned):
    half_sums(core_ref[0], e, rot, cent, codes, assigned, out, turned)


def chip_sums(mine, theirs, out):
    for part in range(mine.shape[0]):

        def add(x, carry):
            out[part, x] = (mine[part, x] + theirs[part, x].astype(f32)).astype(bf16)
            return carry

        lax.fori_loop(0, X, add, 0)


def first_sums(arrived, out):
    def summed(a, b):
        return arrived[:, a:b, :].astype(f32).sum(axis=0)

    grams, books = D // PARTS, K // PARTS
    coarse = summed(grams + books, ROWS // PARTS)
    zeros = jnp.zeros((PART - C0 - CP, LANES), f32)
    for q in range(out.shape[0]):
        out[q, :GP, :] = summed(q * GP, (q + 1) * GP).astype(bf16)
        out[q, GP:C0, :] = summed(grams + q * BP, grams + (q + 1) * BP).astype(bf16)
        mine = coarse[q * CP : (q + 1) * CP, :]
        out[q, C0:PART, :] = jnp.concatenate([mine, zeros], axis=0).astype(bf16)


def second_sums(arrived, out):
    total = arrived[...].astype(f32).sum(axis=0)
    high = total.astype(bf16)
    low = total - high.astype(f32)
    coarse = jnp.concatenate([total[C0 : C0 + 8], low[C0 : C0 + 8]], axis=0).astype(bf16)
    book = low[GP:C0].astype(bf16)
    for i in range(out.shape[0]):
        out[i, :C0, :] = high[:C0]
        out[i, C0:PART, :] = coarse
        out[i, PART:ONE, :] = book


def owned_sums(place_ref, arrived, coarse_out, mine, *, vectors):
    total = arrived[...].astype(f32).sum(axis=0)
    coarse = total[C0 : C0 + 8] + total[C0 + 8 : C0 + 16]
    row = lax.broadcasted_iota(jnp.int32, (8, LANES), 0)
    own = jnp.where(row == place_ref[0], coarse, 0.0).sum(axis=0, keepdims=True)
    coarse_out[...] = own * (CENTS / vectors) ** 0.5
    gram = total[:GP] * (1.0 / vectors)
    book = (total[GP:C0] + total[PART:ONE]) * (K / vectors) ** 0.5

    def scaled(v):
        top = jnp.max(jnp.abs(v), keepdims=True)
        power = jnp.ceil(jnp.log2(jnp.maximum(top, 2.0**-100)))
        return v * jnp.exp2(-power), jnp.broadcast_to(power, (8, LANES))

    gram, gram_power = scaled(gram)
    book, book_power = scaled(book)
    mine[:GP, :] = gram
    mine[GP:C0, :] = book
    mine[C0:SPREAD, :] = jnp.where(row == 0, gram_power, book_power)


def laid_out(arrived, gram, book):
    for q in range(PEERS):
        power = jnp.exp2(arrived[q, C0:SPREAD, :])
        j, top = q * GP // LANES, q * GP % LANES
        gram[top : top + GP, j * LANES : (j + 1) * LANES] = arrived[q, :GP, :] * power[0:1]
        book[q * BP : (q + 1) * BP, :] = arrived[q, GP:C0, :] * power[1:2]


def per_device(embeddings, rotation, centroids, assignments, codes):
    rows = embeddings.shape[0]
    vectors = rows * lax.axis_size(DP_SUB)
    core = lax.axis_index("c").reshape(1)
    place = lax.axis_index("zs").reshape(1)
    inputs = (embeddings, rotation, centroids, codes.T, assignments)
    inputs = tuple(pltpu.with_memory_space_constraint(v, pltpu.HBM) for v in inputs)
    shape = (PARTS, X, ROWS // PARTS, LANES)
    turned = pltpu.VMEM((X * LANES, rows), bf16)
    theirs, *held = pl.pallas_call(
        sibling_sums,
        out_shape=[jax.ShapeDtypeStruct(shape, bf16)]
        + [jax.ShapeDtypeStruct(v.shape, v.dtype) for v in inputs],
        in_specs=[SMEM] * 2 + [HBM] * 5,
        out_specs=[VMEM] * 6,
        scratch_shapes=[turned, pltpu.SemaphoreType.DMA((5,))],
        compiler_params=params(24),
        name="sibling_sums",
    )(core, place, *inputs)
    arrived = lax.ppermute(theirs, "c", [(0, 1), (1, 0)])
    mine = pl.pallas_call(
        own_sums,
        out_shape=jax.ShapeDtypeStruct(shape, f32),
        in_specs=[SMEM] + [VMEM] * 5,
        out_specs=VMEM,
        scratch_shapes=[turned],
        compiler_params=params(24),
        cost_estimate=pl.CostEstimate(flops=4 * 10**9, bytes_accessed=8 * 10**6, transcendentals=0),
        name="own_sums",
    )(core, *held)
    parts = pl.pallas_call(
        chip_sums,
        out_shape=jax.ShapeDtypeStruct(shape, bf16),
        in_specs=[VMEM] * 2,
        out_specs=VMEM,
        compiler_params=params(16),
        name="chip_sums",
    )(mine, arrived)
    parts = parts.reshape(PARTS * X, ROWS // PARTS, LANES)
    arrived = lax.all_to_all(parts, NEAR + ("x",), split_axis=0, concat_axis=0, tiled=True)
    pieces = pl.pallas_call(
        first_sums,
        out_shape=jax.ShapeDtypeStruct((PEERS // PARTS, PART, LANES), bf16),
        in_specs=[VMEM],
        out_specs=VMEM,
        compiler_params=params(16),
        name="first_sums",
    )(arrived)
    arrived = lax.all_to_all(pieces, FAR, split_axis=0, concat_axis=0, tiled=True)
    pieces = pl.pallas_call(
        second_sums,
        out_shape=jax.ShapeDtypeStruct((ZS, ONE, LANES), bf16),
        in_specs=[VMEM],
        out_specs=VMEM,
        compiler_params=params(16),
        name="second_sums",
    )(arrived)
    arrived = lax.all_to_all(pieces, "zs", split_axis=0, concat_axis=0, tiled=True)
    coarse_sums, mine = pl.pallas_call(
        lambda *refs: owned_sums(*refs, vectors=vectors),
        out_shape=(
            jax.ShapeDtypeStruct((1, LANES), f32),
            jax.ShapeDtypeStruct((SPREAD, LANES), f32),
        ),
        in_specs=[SMEM, VMEM],
        out_specs=(VMEM, VMEM),
        compiler_params=params(16),
        name="owned_sums",
    )(place, arrived)
    spread = jnp.broadcast_to(mine.astype(f16)[None], (PEERS, SPREAD, LANES))
    arrived = lax.all_to_all(spread, OWNERS, split_axis=0, concat_axis=0, tiled=True)
    gram, codebook_sums = pl.pallas_call(
        laid_out,
        out_shape=(jax.ShapeDtypeStruct((LANES, D), f32), jax.ShapeDtypeStruct((K, LANES), f32)),
        in_specs=[VMEM],
        out_specs=(VMEM, VMEM),
        compiler_params=params(16),
        name="laid_out",
    )(arrived.astype(f32))
    return gram, coarse_sums, codebook_sums


def solution(mesh):
    finer = Mesh(mesh.devices.reshape(ZS, ZF, YS, YF, X, 2), DP_SUB)
    return jax.shard_map(
        per_device,
        mesh=finer,
        in_specs=(P(DP_SUB, None), P(), P(), P(DP_SUB), P(DP_SUB, None)),
        out_specs=(P(("x", "c"), None), P(DP, ("x", "c")), P(None, ("x", "c"))),
        check_vma=False,
    )
```

time: 107 us -> 96.6 us (0.903)
  local copies, waits for them, and re-layouts: 4.48 us -> 0.05 us
  blocking collectives: 84.8 us -> 80.5 us
  Pallas kernels: 10.1 us -> 13.1 us
  starting transfers between devices: 4.33 us -> 1.92 us
    unnamed x6 -> x0, local copies, waits for them, and re-layouts: 3.74 us -> none
    all_to_all x2, blocking collectives: 46.6 us -> 43.4 us  [the longest x1 26.2 us: per_device(): lax.all_to_all(parts, NEAR + ('x',), split_axis=0, concat_axis=0, tiled=T...]
    pallas_call x2 -> x4, Pallas kernels: 8.63 us -> 11.6 us  [the longest x1 6.29 us: per_device(): pl.pallas_call(sibling_sums, out_shape=[jax.ShapeDtypeStruct(shape, bf16)...]
    ppermute x2 -> x1, starting transfers between devices: 4.33 us -> 1.92 us  [per_device(): arrived = lax.ppermute(theirs, 'c', [(0, 1), (1, 0)])]
    all_to_all x1, blocking collectives: 14.9 us -> 13.7 us  [per_device(): lax.all_to_all(spread, OWNERS, split_axis=0, concat_axis=0, tiled=True)]
  transfers between devices with their start and end apart: 2 -> 1, of which waited for: 1 -> 0; matrix products, arithmetic and copies ran while one was open for 2% -> 0% of each run, Pallas kernels for 0% -> 5%
where the time goes in v5:
time: 96.6 us; the launch traced here: 96.3 us
  blocking collectives  80.5 us (83%)
  Pallas kernels  13.1 us (14%)
  starting transfers between devices  1.92 us (2%)
    all_to_all x1, blocking collectives, per_device(): lax.all_to_all(parts, NEAR + ('x',), split_axis=0, concat_axis=0, tiled=T...  26.2 us
    all_to_all x1, blocking collectives, per_device(): lax.all_to_all(pieces, 'zs', split_axis=0, concat_axis=0, tiled=True)  23.4 us
    all_to_all x1, blocking collectives, per_device(): lax.all_to_all(pieces, FAR, split_axis=0, concat_axis=0, tiled=True)  17.3 us
    all_to_all x1, blocking collectives, per_device(): lax.all_to_all(spread, OWNERS, split_axis=0, concat_axis=0, tiled=True)  13.7 us
    pallas_call x1, Pallas kernels, per_device(): pl.pallas_call(sibling_sums, out_shape=[jax.ShapeDtypeStruct(shape, bf16)...  6.29 us
    pallas_call x1, Pallas kernels, per_device(): pl.pallas_call(own_sums, out_shape=jax.ShapeDtypeStruct(shape, f32), in_s...  4.82 us
  transfers between devices with their start and end apart: 1, of which 0 were waited for; matrix products, arithmetic and copies ran while one was open for 0% of the time, Pallas kernels for 5%

profile of v5, /device:TPU:8, one launch (start us, length us, event | category | flops | bytes accessed | tf_op | source)
XLA Modules:
  0.0 96.3 jit_solution(16920119968316642289)
XLA Ops:
  0.6 6.3 %sibling_sums.1 = (bf16[2,4,688,128]{3,2,1,0:T(8,128)(2,1)S(1)}, bf16[512,1024]{1,0:T(8,128)(2,1)S(1)}, bf16[1024,1024]{1,0:T(8,128)(2,1)S(1)}, bf16[96,1024]{1,...) custom-call(s32[1]{0:T(128)} %bitcast.1.core_ref, s32[1]{0:T(128)} %bitcast.place_ref.refs_0_, ...), custom_call_target="tpu_custom_call" | custom-call | tf_op jit(solution)/shard_map/sibling_sums/pallas_call | solution.py:207
  6.9 1.9 %collective-permute-start = (bf16[2,4,688,128]{3,2,1,0:T(8,128)(2,1)S(1)}, bf16[2,4,688,128]{3,2,1,0:T(8,128)(2,1)S(1)}, u32[]{:S(2)}, u32[]{:S(2)}) collective-permute-start(bf16[2,4,688,128]{3,2,1,0:T(8,128)(2,1)S(1)} %get-tuple-element.18), channel_id=1, source_target_pairs={{0,1},{1,0},{2,3},{3,2},{4,5},{5,4},{6,7},{7,6},{8,9},{9,8},{10,11... | collective-permute-start | bytes 4227080 | tf_op jit(solution)/shard_map/ppermute | solution.py:217
  8.9 4.8 %own_sums.1.mine = f32[2,4,688,128]{3,2,1,0:T(8,128)S(1)} custom-call(s32[1]{0:T(128)} %bitcast.1.core_ref, bf16[512,1024]{1,0:T(8,128)(2,1)S(1)} %get-tuple-element.13.e, bf16[1024,1024]{1,0:T(8,128)(2,1)S(1)} %get-tuple-element.14.rot, bf16[96,1024]{1,0:T(8,128)(2,1)S(1)} %get-tuple-element.15.cent, s32[64,512]{1,0:T(8,128)S(1)} %get-tuple-element.16.codes, ...), custom_call_target="tpu_custom_call" | custom-call | flops 4000000000 | bytes 8000000 | tf_op jit(solution)/shard_map/own_sums/pallas_call | solution.py:218
  13.7 0.0 collective-permute-done.theirs
  13.7 0.3 chip_sums.1
  14.0 26.2 %all_to_all.20.arrived = bf16[8,688,128]{2,1,0:T(8,128)(2,1)S(1)} all-to-all(bf16[8,688,128]{2,1,0:T(8,128)(2,1)S(1)} %bitcast.4), channel_id=1, replica_groups=mesh['zs'=6,'zf'=2,'ys'=4,'yf'=2,'x'=4,'c'=2] {'zf','x'}, dimensions={0} | all-to-all | bytes 2818048 | tf_op jit(solution)/shard_map/all_to_all | solution.py:237
  40.2 0.2 first_sums.1
  40.4 17.3 %all_to_all.21.arrived = bf16[8,96,128]{2,1,0:T(8,128)(2,1)S(1)} all-to-all(bf16[8,96,128]{2,1,0:T(8,128)(2,1)S(1)} %first_sums.1), channel_id=1, replica_groups=mesh['zs'=6,'zf'=2,'ys'=4,'yf'=2,'x'=4,'c'=2] {'yf','ys'}, dimensions={0} | all-to-all | bytes 393216 | tf_op jit(solution)/shard_map/all_to_all | solution.py:246
  57.7 23.4 %all_to_all.22.refs_1_ = bf16[6,112,128]{2,1,0:T(8,128)(2,1)S(1)} all-to-all(bf16[6,112,128]{2,1,0:T(8,128)(2,1)S(1)} %second_sums.1), channel_id=1, replica_groups=mesh['zs'=6,'zf'=2,'ys'=4,'yf'=2,'x'=4,'c'=2] {'zs'}, dimensions={0} | all-to-all | bytes 344064 | tf_op jit(solution)/shard_map/all_to_all | solution.py:255
  81.1 0.5 owned_sums.1
  81.6 0.1 broadcast_in_dim.2
  81.7 13.7 %all_to_all.23 = f16[16,88,128]{2,1,0:T(8,128)(2,1)S(1)} all-to-all(f16[16,88,128]{2,1,0:T(8,128)(2,1)S(1)} %broadcast_in_dim.2), channel_id=1, replica_groups=mesh['zs'=6,'zf'=2,'ys'=4,'yf'=2,'x'=4,'c'=2] {'zf','yf','ys'}, dimensions={0} | all-to-all | bytes 720896 | tf_op jit(solution)/shard_map/all_to_all | solution.py:268
  95.4 0.9 laid_out.1
  (3 shorter events, 0.1 us)
Async XLA Ops:
  6.9 6.8 %collective-permute-start = (bf16[2,4,688,128]{3,2,1,0:T(8,128)(2,1)S(1)}, bf16[2,4,688,128]{3,2,1,0:T(8,128)(2,1)S(1)}, u32[]{:S(2)}, u32[]{:S(2)}) collective-permute-start(bf16[2,4,688,128]{3,2,1,0:T(8,128)(2,1)S(1)} %get-tuple-element.18), channel_id=1, source_target_pairs={{0,1},{1,0},{2,3},{3,2},{4,5},{5,4},{6,7},{7,6},{8,9},{9,8},{10,11... | collective-permute-start | bytes 4227080 | tf_op jit(solution)/shard_map/ppermute | solution.py:217

commit v6 on v5

--- a/solution.py
+++ b/solution.py
@@ -12,6 +12,7 @@
 CENTS = 96
 LANES = 128
 SUBS = 8
+GROUPS = 4
 X = 4
 YS = 4
 YF = 2
@@ -56,14 +57,28 @@
 
 def book_sums(res, codes):
     rows = res.shape[0]
-    word = lax.broadcasted_iota(jnp.int32, (K, rows), 0)
-    lane = lax.broadcasted_iota(jnp.int32, (rows, LANES), 1)
-    total = jnp.zeros((K, LANES), f32)
-    for m in range(SUBS):
-        onehot = (word == codes[m : m + 1, :]).astype(bf16)
-        part = jnp.where(lane // (LANES // SUBS) == m, res, jnp.zeros_like(res))
-        total += dot(onehot, part)
-    return total
+    low_words = K // GROUPS
+    group = lax.shift_right_logical(codes, low_words.bit_length() - 1)
+    low = codes - group * low_words
+    sub = lax.broadcasted_iota(jnp.int32, (SUBS, LANES), 0)
+    lane = lax.broadcasted_iota(jnp.int32, (SUBS, LANES), 1)
+    select = (lane // (LANES // SUBS) == sub).astype(f32).astype(bf16)
+    group = group.astype(f32).astype(bf16)
+    which = lax.dot_general(group, select, (((0,), (0,)), ((), ())), preferred_element_type=f32)
+    zeros = jnp.zeros_like(res)
+    spread = jnp.concatenate([jnp.where(which == g, res, zeros) for g in range(GROUPS)], axis=1)
+    word = lax.broadcasted_iota(jnp.int32, (low_words, rows), 0)
+    onehot = [(word == low[m : m + 1, :]).astype(bf16) for m in range(SUBS)]
+    sums = dot(jnp.concatenate(onehot, axis=0), spread)
+    mine = lax.broadcasted_iota(jnp.int32, (low_words, LANES), 1) // (LANES // SUBS)
+    totals = []
+    for g in range(GROUPS):
+        total = jnp.zeros((low_words, LANES), f32)
+        for m in range(SUBS):
+            part = sums[m * low_words : (m + 1) * low_words, g * LANES : (g + 1) * LANES]
+            total = jnp.where(mine == m, part, total)
+        totals.append(total)
+    return jnp.concatenate(totals, axis=0)
 
 
 def half_sums(whose, e, rot, cent, codes, assigned, out, turned, wait=None):

time: 96.6 us -> 94.4 us (0.977)
  Pallas kernels: 13.1 us -> 10.9 us
    pallas_call x1, Pallas kernels: 6.29 us -> 5.14 us  [per_device(): pl.pallas_call(sibling_sums, out_shape=[jax.ShapeDtypeStruct(shape, bf16)...]
    pallas_call x1, Pallas kernels: 4.82 us -> 3.72 us  [per_device(): pl.pallas_call(own_sums, out_shape=jax.ShapeDtypeStruct(shape, f32), in_s...]
  transfers between devices with their start and end apart: 1 -> 1, of which waited for: 0 -> 0; matrix products, arithmetic and copies ran while one was open for 0% -> 0% of each run, Pallas kernels for 5% -> 4%
where the time goes in v6:
time: 94.4 us; the launch traced here: 94.1 us
  blocking collectives  80.5 us (85%)
  Pallas kernels  10.9 us (12%)
  starting transfers between devices  1.92 us (2%)
    all_to_all x1, blocking collectives, per_device(): lax.all_to_all(parts, NEAR + ('x',), split_axis=0, concat_axis=0, tiled=T...  26.2 us
    all_to_all x1, blocking collectives, per_device(): lax.all_to_all(pieces, 'zs', split_axis=0, concat_axis=0, tiled=True)  23.4 us
    all_to_all x1, blocking collectives, per_device(): lax.all_to_all(pieces, FAR, split_axis=0, concat_axis=0, tiled=True)  17.3 us
    all_to_all x1, blocking collectives, per_device(): lax.all_to_all(spread, OWNERS, split_axis=0, concat_axis=0, tiled=True)  13.7 us
    pallas_call x1, Pallas kernels, per_device(): pl.pallas_call(sibling_sums, out_shape=[jax.ShapeDtypeStruct(shape, bf16)...  5.14 us
    pallas_call x1, Pallas kernels, per_device(): pl.pallas_call(own_sums, out_shape=jax.ShapeDtypeStruct(shape, f32), in_s...  3.72 us
    ppermute x1, starting transfers between devices, per_device(): arrived = lax.ppermute(theirs, 'c', [(0, 1), (1, 0)])  1.92 us
  transfers between devices with their start and end apart: 1, of which 0 were waited for; matrix products, arithmetic and copies ran while one was open for 0% of the time, Pallas kernels for 4%

profile of v6, /device:TPU:8, one launch (start us, length us, event | category | flops | bytes accessed | tf_op | source)
XLA Modules:
  0.0 94.1 jit_solution(14562855546125809587)
XLA Ops:
  0.6 5.1 %sibling_sums.1 = (bf16[2,4,688,128]{3,2,1,0:T(8,128)(2,1)S(1)}, bf16[512,1024]{1,0:T(8,128)(2,1)S(1)}, bf16[1024,1024]{1,0:T(8,128)(2,1)S(1)}, bf16[96,1024]{1,...) custom-call(s32[1]{0:T(128)} %bitcast.1.core_ref, s32[1]{0:T(128)} %bitcast.place_ref.refs_0_, ...), custom_call_target="tpu_custom_call" | custom-call | tf_op jit(solution)/shard_map/sibling_sums/pallas_call | solution.py:222
  5.8 1.9 %collective-permute-start = (bf16[2,4,688,128]{3,2,1,0:T(8,128)(2,1)S(1)}, bf16[2,4,688,128]{3,2,1,0:T(8,128)(2,1)S(1)}, u32[]{:S(2)}, u32[]{:S(2)}) collective-permute-start(bf16[2,4,688,128]{3,2,1,0:T(8,128)(2,1)S(1)} %get-tuple-element.18), channel_id=1, source_target_pairs={{0,1},{1,0},{2,3},{3,2},{4,5},{5,4},{6,7},{7,6},{8,9},{9,8},{10,11... | collective-permute-start | bytes 4227080 | tf_op jit(solution)/shard_map/ppermute | solution.py:232
  7.7 3.7 %own_sums.1.mine = f32[2,4,688,128]{3,2,1,0:T(8,128)S(1)} custom-call(s32[1]{0:T(128)} %bitcast.1.core_ref, bf16[512,1024]{1,0:T(8,128)(2,1)S(1)} %get-tuple-element.13.e, bf16[1024,1024]{1,0:T(8,128)(2,1)S(1)} %get-tuple-element.14.rot, bf16[96,1024]{1,0:T(8,128)(2,1)S(1)} %get-tuple-element.15.cent, s32[64,512]{1,0:T(8,128)S(1)} %get-tuple-element.16.codes, ...), custom_call_target="tpu_custom_call" | custom-call | flops 4000000000 | bytes 8000000 | tf_op jit(solution)/shard_map/own_sums/pallas_call | solution.py:233
  11.4 0.0 collective-permute-done.theirs
  11.5 0.3 chip_sums.1
  11.8 26.2 %all_to_all.20.arrived = bf16[8,688,128]{2,1,0:T(8,128)(2,1)S(1)} all-to-all(bf16[8,688,128]{2,1,0:T(8,128)(2,1)S(1)} %bitcast.4), channel_id=1, replica_groups=mesh['zs'=6,'zf'=2,'ys'=4,'yf'=2,'x'=4,'c'=2] {'zf','x'}, dimensions={0} | all-to-all | bytes 2818048 | tf_op jit(solution)/shard_map/all_to_all | solution.py:252
  38.0 0.2 first_sums.1
  38.1 17.3 %all_to_all.21.arrived = bf16[8,96,128]{2,1,0:T(8,128)(2,1)S(1)} all-to-all(bf16[8,96,128]{2,1,0:T(8,128)(2,1)S(1)} %first_sums.1), channel_id=1, replica_groups=mesh['zs'=6,'zf'=2,'ys'=4,'yf'=2,'x'=4,'c'=2] {'yf','ys'}, dimensions={0} | all-to-all | bytes 393216 | tf_op jit(solution)/shard_map/all_to_all | solution.py:261
  55.4 23.4 %all_to_all.22.refs_1_ = bf16[6,112,128]{2,1,0:T(8,128)(2,1)S(1)} all-to-all(bf16[6,112,128]{2,1,0:T(8,128)(2,1)S(1)} %second_sums.1), channel_id=1, replica_groups=mesh['zs'=6,'zf'=2,'ys'=4,'yf'=2,'x'=4,'c'=2] {'zs'}, dimensions={0} | all-to-all | bytes 344064 | tf_op jit(solution)/shard_map/all_to_all | solution.py:270
  78.9 0.5 owned_sums.1
  79.4 0.1 broadcast_in_dim.2
  79.5 13.7 %all_to_all.23 = f16[16,88,128]{2,1,0:T(8,128)(2,1)S(1)} all-to-all(f16[16,88,128]{2,1,0:T(8,128)(2,1)S(1)} %broadcast_in_dim.2), channel_id=1, replica_groups=mesh['zs'=6,'zf'=2,'ys'=4,'yf'=2,'x'=4,'c'=2] {'zf','yf','ys'}, dimensions={0} | all-to-all | bytes 720896 | tf_op jit(solution)/shard_map/all_to_all | solution.py:283
  93.2 0.9 laid_out.1
  (3 shorter events, 0.1 us)
Async XLA Ops:
  5.8 5.7 %collective-permute-start = (bf16[2,4,688,128]{3,2,1,0:T(8,128)(2,1)S(1)}, bf16[2,4,688,128]{3,2,1,0:T(8,128)(2,1)S(1)}, u32[]{:S(2)}, u32[]{:S(2)}) collective-permute-start(bf16[2,4,688,128]{3,2,1,0:T(8,128)(2,1)S(1)} %get-tuple-element.18), channel_id=1, source_target_pairs={{0,1},{1,0},{2,3},{3,2},{4,5},{5,4},{6,7},{7,6},{8,9},{9,8},{10,11... | collective-permute-start | bytes 4227080 | tf_op jit(solution)/shard_map/ppermute | solution.py:232

commit v7 on v6

--- a/solution.py
+++ b/solution.py
@@ -13,6 +13,7 @@
 LANES = 128
 SUBS = 8
 GROUPS = 4
+CHUNKS = 2
 X = 4
 YS = 4
 YF = 2
@@ -81,11 +82,16 @@
     return jnp.concatenate(totals, axis=0)
 
 
-def half_sums(whose, e, rot, cent, codes, assigned, out, turned, wait=None):
+def half_sums(whose, e, rot, cent, codes, assigned, out, turned, arrive=None, wait=None):
     rows = e.shape[0]
-    for x in range(X):
-        turned[x * LANES : (x + 1) * LANES, :] = e[:, columns(whose, x)].T
-    wide = 256
+    step = rows // CHUNKS
+    for i in range(CHUNKS):
+        if arrive is not None:
+            arrive(i)
+        here = slice(i * step, (i + 1) * step)
+        for x in range(X):
+            turned[x * LANES : (x + 1) * LANES, here] = e[here, columns(whose, x)].T
+    wide = 512
     grams, books, cents = D // PARTS, K // PARTS, CENTS // PARTS
     book0, coarse0 = grams, grams + books
     for n in range(D // wide):
@@ -105,40 +111,46 @@
     named = assigned[...].reshape(1, rows)
     pick = (label == named).astype(bf16)
     send = (sent == named).astype(bf16)
-    for q in range(X // 2):
-        pair = (columns(whose, 2 * q), columns(whose, 2 * q + 1))
-        c = jnp.concatenate([cent[:, p] for p in pair], axis=1)
-        r = jnp.concatenate([rot[:, p] for p in pair], axis=1)
-        base = lax.dot_general(pick, c, (((0,), (0,)), ((), ())), preferred_element_type=f32)
-        residual = (dot(e[...], r) - base).astype(bf16)
-        coarse = dot(send, residual).astype(out.dtype)
-        for k in range(2):
-            x = 2 * q + k
-            lanes = slice(k * LANES, (k + 1) * LANES)
-            subs = pl.ds(pl.multiple_of((2 * x + whose) * SUBS, SUBS), SUBS)
-            total = book_sums(residual[:, lanes], codes[subs, :]).astype(out.dtype)
-            for part in range(PARTS):
-                out[part, x, book0:coarse0, :] = total[part * books : (part + 1) * books]
-                out[part, x, coarse0:, :] = coarse[part * cents : (part + 1) * cents, lanes]
+    lanes_of = [columns(whose, x) for x in range(X)]
+    c = jnp.concatenate([cent[:, p] for p in lanes_of], axis=1)
+    r = jnp.concatenate([rot[:, p] for p in lanes_of], axis=1)
+    base = lax.dot_general(pick, c, (((0,), (0,)), ((), ())), preferred_element_type=f32)
+    residual = (dot(e[...], r) - base).astype(bf16)
+    coarse = dot(send, residual).astype(out.dtype)
+    for x in range(X):
+        lanes = slice(x * LANES, (x + 1) * LANES)
+        subs = pl.ds(pl.multiple_of((2 * x + whose) * SUBS, SUBS), SUBS)
+        total = book_sums(residual[:, lanes], codes[subs, :]).astype(out.dtype)
+        for part in range(PARTS):
+            out[part, x, book0:coarse0, :] = total[part * books : (part + 1) * books]
+            out[part, x, coarse0:, :] = coarse[part * cents : (part + 1) * cents, lanes]
 
 
 def sibling_sums(
     core_ref, place_ref, e_in, rot_in, cent_in, codes_in, assigned_in,
     out, e, rot, cent, codes, assigned, turned, sems,
 ):
-    pairs = (
-        (e_in, e), (assigned_in, assigned), (cent_in, cent), (codes_in, codes), (rot_in, rot),
-    )
-    copies = [pltpu.make_async_copy(a, b, sems.at[i]) for i, (a, b) in enumerate(pairs)]
-    for copy in copies:
+    step = e.shape[0] // CHUNKS
+    first = []
+    for i in range(CHUNKS):
+        here = slice(i * step, (i + 1) * step)
+        first.append(pltpu.make_async_copy(e_in.at[here], e.at[here], sems.at[i]))
+    pairs = ((assigned_in, assigned), (cent_in, cent), (codes_in, codes), (rot_in, rot))
+    copies = [pltpu.make_async_copy(a, b, sems.at[CHUNKS + i]) for i, (a, b) in enumerate(pairs)]
+    for copy in first:
         copy.start()
-    copies[0].wait()
+
+    def arrive(i):
+        first[i].wait()
+        if i == 0:
+            for copy in copies:
+                copy.start()
 
     def wait():
-        for copy in copies[1:]:
+        for copy in copies:
             copy.wait()
 
-    half_sums(1 - core_ref[0], e, rot, cent, codes, assigned, out, turned, wait)
+    half_sums(1 - core_ref[0], e, rot, cent, codes, assigned, out, turned, arrive, wait)
 
 
 def own_sums(core_ref, e, rot, cent, codes, assigned, out, turned):
@@ -225,7 +237,7 @@
         + [jax.ShapeDtypeStruct(v.shape, v.dtype) for v in inputs],
         in_specs=[SMEM] * 2 + [HBM] * 5,
         out_specs=[VMEM] * 6,
-        scratch_shapes=[turned, pltpu.SemaphoreType.DMA((5,))],
+        scratch_shapes=[turned, pltpu.SemaphoreType.DMA((CHUNKS + 4,))],
         compiler_params=params(24),
         name="sibling_sums",
     )(core, place, *inputs)

time: 94.4 us -> 95 us (level)
  no operation moved by 1% of the time
where the time goes in v7:
time: 95 us; the launch traced here: 94.7 us
  blocking collectives  80.5 us (85%)
  Pallas kernels  11.4 us (12%)
  starting transfers between devices  1.92 us (2%)
    all_to_all x1, blocking collectives, per_device(): lax.all_to_all(parts, NEAR + ('x',), split_axis=0, concat_axis=0, tiled=T...  26.2 us
    all_to_all x1, blocking collectives, per_device(): lax.all_to_all(pieces, 'zs', split_axis=0, concat_axis=0, tiled=True)  23.4 us
    all_to_all x1, blocking collectives, per_device(): lax.all_to_all(pieces, FAR, split_axis=0, concat_axis=0, tiled=True)  17.3 us
    all_to_all x1, blocking collectives, per_device(): lax.all_to_all(spread, OWNERS, split_axis=0, concat_axis=0, tiled=True)  13.7 us
    pallas_call x1, Pallas kernels, per_device(): pl.pallas_call(sibling_sums, out_shape=[jax.ShapeDtypeStruct(shape, bf16)...  5.85 us
    pallas_call x1, Pallas kernels, per_device(): pl.pallas_call(own_sums, out_shape=jax.ShapeDtypeStruct(shape, f32), in_s...  3.55 us
    ppermute x1, starting transfers between devices, per_device(): arrived = lax.ppermute(theirs, 'c', [(0, 1), (1, 0)])  1.92 us
  transfers between devices with their start and end apart: 1, of which 0 were waited for; matrix products, arithmetic and copies ran while one was open for 0% of the time, Pallas kernels for 4%

profile of v7, /device:TPU:8, one launch (start us, length us, event | category | flops | bytes accessed | tf_op | source)
XLA Modules:
  0.0 94.7 jit_solution(13878463647109962318)
XLA Ops:
  0.6 5.9 %sibling_sums.1 = (bf16[2,4,688,128]{3,2,1,0:T(8,128)(2,1)S(1)}, bf16[512,1024]{1,0:T(8,128)(2,1)S(1)}, bf16[1024,1024]{1,0:T(8,128)(2,1)S(1)}, bf16[96,1024]{1,...) custom-call(s32[1]{0:T(128)} %bitcast.1.core_ref, s32[1]{0:T(128)} %bitcast.place_ref.refs_0_, ...), custom_call_target="tpu_custom_call" | custom-call | tf_op jit(solution)/shard_map/sibling_sums/pallas_call | solution.py:234
  6.5 1.9 %collective-permute-start = (bf16[2,4,688,128]{3,2,1,0:T(8,128)(2,1)S(1)}, bf16[2,4,688,128]{3,2,1,0:T(8,128)(2,1)S(1)}, u32[]{:S(2)}, u32[]{:S(2)}) collective-permute-start(bf16[2,4,688,128]{3,2,1,0:T(8,128)(2,1)S(1)} %get-tuple-element.18), channel_id=1, source_target_pairs={{0,1},{1,0},{2,3},{3,2},{4,5},{5,4},{6,7},{7,6},{8,9},{9,8},{10,11... | collective-permute-start | bytes 4227080 | tf_op jit(solution)/shard_map/ppermute | solution.py:244
  8.4 3.6 %own_sums.1.mine = f32[2,4,688,128]{3,2,1,0:T(8,128)S(1)} custom-call(s32[1]{0:T(128)} %bitcast.1.core_ref, bf16[512,1024]{1,0:T(8,128)(2,1)S(1)} %get-tuple-element.13.e, bf16[1024,1024]{1,0:T(8,128)(2,1)S(1)} %get-tuple-element.14.rot, bf16[96,1024]{1,0:T(8,128)(2,1)S(1)} %get-tuple-element.15.cent, s32[64,512]{1,0:T(8,128)S(1)} %get-tuple-element.16.codes, ...), custom_call_target="tpu_custom_call" | custom-call | flops 4000000000 | bytes 8000000 | tf_op jit(solution)/shard_map/own_sums/pallas_call | solution.py:245
  12.0 0.0 collective-permute-done.theirs
  12.0 0.3 chip_sums.1
  12.3 26.2 %all_to_all.20.arrived = bf16[8,688,128]{2,1,0:T(8,128)(2,1)S(1)} all-to-all(bf16[8,688,128]{2,1,0:T(8,128)(2,1)S(1)} %bitcast.4), channel_id=1, replica_groups=mesh['zs'=6,'zf'=2,'ys'=4,'yf'=2,'x'=4,'c'=2] {'zf','x'}, dimensions={0} | all-to-all | bytes 2818048 | tf_op jit(solution)/shard_map/all_to_all | solution.py:264
  38.5 0.2 first_sums.1
  38.7 17.3 %all_to_all.21.arrived = bf16[8,96,128]{2,1,0:T(8,128)(2,1)S(1)} all-to-all(bf16[8,96,128]{2,1,0:T(8,128)(2,1)S(1)} %first_sums.1), channel_id=1, replica_groups=mesh['zs'=6,'zf'=2,'ys'=4,'yf'=2,'x'=4,'c'=2] {'yf','ys'}, dimensions={0} | all-to-all | bytes 393216 | tf_op jit(solution)/shard_map/all_to_all | solution.py:273
  56.0 23.4 %all_to_all.22.refs_1_ = bf16[6,112,128]{2,1,0:T(8,128)(2,1)S(1)} all-to-all(bf16[6,112,128]{2,1,0:T(8,128)(2,1)S(1)} %second_sums.1), channel_id=1, replica_groups=mesh['zs'=6,'zf'=2,'ys'=4,'yf'=2,'x'=4,'c'=2] {'zs'}, dimensions={0} | all-to-all | bytes 344064 | tf_op jit(solution)/shard_map/all_to_all | solution.py:282
  79.4 0.5 owned_sums.1
  80.0 0.1 broadcast_in_dim.2
  80.0 13.7 %all_to_all.23 = f16[16,88,128]{2,1,0:T(8,128)(2,1)S(1)} all-to-all(f16[16,88,128]{2,1,0:T(8,128)(2,1)S(1)} %broadcast_in_dim.2), channel_id=1, replica_groups=mesh['zs'=6,'zf'=2,'ys'=4,'yf'=2,'x'=4,'c'=2] {'zf','yf','ys'}, dimensions={0} | all-to-all | bytes 720896 | tf_op jit(solution)/shard_map/all_to_all | solution.py:295
  93.8 0.9 laid_out.1
  (3 shorter events, 0.1 us)
Async XLA Ops:
  6.5 5.5 %collective-permute-start = (bf16[2,4,688,128]{3,2,1,0:T(8,128)(2,1)S(1)}, bf16[2,4,688,128]{3,2,1,0:T(8,128)(2,1)S(1)}, u32[]{:S(2)}, u32[]{:S(2)}) collective-permute-start(bf16[2,4,688,128]{3,2,1,0:T(8,128)(2,1)S(1)} %get-tuple-element.18), channel_id=1, source_target_pairs={{0,1},{1,0},{2,3},{3,2},{4,5},{5,4},{6,7},{7,6},{8,9},{9,8},{10,11... | collective-permute-start | bytes 4227080 | tf_op jit(solution)/shard_map/ppermute | solution.py:244

commit v8 on v7

--- a/solution.py
+++ b/solution.py
@@ -13,7 +13,7 @@
 LANES = 128
 SUBS = 8
 GROUPS = 4
-CHUNKS = 2
+CHUNKS = 1
 X = 4
 YS = 4
 YF = 2
@@ -130,24 +130,16 @@
     core_ref, place_ref, e_in, rot_in, cent_in, codes_in, assigned_in,
     out, e, rot, cent, codes, assigned, turned, sems,
 ):
-    step = e.shape[0] // CHUNKS
-    first = []
-    for i in range(CHUNKS):
-        here = slice(i * step, (i + 1) * step)
-        first.append(pltpu.make_async_copy(e_in.at[here], e.at[here], sems.at[i]))
-    pairs = ((assigned_in, assigned), (cent_in, cent), (codes_in, codes), (rot_in, rot))
-    copies = [pltpu.make_async_copy(a, b, sems.at[CHUNKS + i]) for i, (a, b) in enumerate(pairs)]
-    for copy in first:
+    pairs = ((e_in, e), (assigned_in, assigned), (cent_in, cent), (codes_in, codes), (rot_in, rot))
+    copies = [pltpu.make_async_copy(a, b, sems.at[i]) for i, (a, b) in enumerate(pairs)]
+    for copy in copies:
         copy.start()
 
     def arrive(i):
-        first[i].wait()
-        if i == 0:
-            for copy in copies:
-                copy.start()
+        copies[0].wait()
 
     def wait():
-        for copy in copies:
+        for copy in copies[1:]:
             copy.wait()
 
     half_sums(1 - core_ref[0], e, rot, cent, codes, assigned, out, turned, arrive, wait)
@@ -237,7 +229,7 @@
         + [jax.ShapeDtypeStruct(v.shape, v.dtype) for v in inputs],
         in_specs=[SMEM] * 2 + [HBM] * 5,
         out_specs=[VMEM] * 6,
-        scratch_shapes=[turned, pltpu.SemaphoreType.DMA((CHUNKS + 4,))],
+        scratch_shapes=[turned, pltpu.SemaphoreType.DMA((12,))],
         compiler_params=params(24),
         name="sibling_sums",
     )(core, place, *inputs)

time: 95 us -> 94.2 us (level)
  no operation moved by 1% of the time
where the time goes in v8:
time: 94.2 us; the launch traced here: 93.9 us
  blocking collectives  80.5 us (85%)
  Pallas kernels  10.7 us (11%)
  starting transfers between devices  1.92 us (2%)
    all_to_all x1, blocking collectives, per_device(): lax.all_to_all(parts, NEAR + ('x',), split_axis=0, concat_axis=0, tiled=T...  26.2 us
    all_to_all x1, blocking collectives, per_device(): lax.all_to_all(pieces, 'zs', split_axis=0, concat_axis=0, tiled=True)  23.4 us
    all_to_all x1, blocking collectives, per_device(): lax.all_to_all(pieces, FAR, split_axis=0, concat_axis=0, tiled=True)  17.3 us
    all_to_all x1, blocking collectives, per_device(): lax.all_to_all(spread, OWNERS, split_axis=0, concat_axis=0, tiled=True)  13.7 us
    pallas_call x1, Pallas kernels, per_device(): pl.pallas_call(sibling_sums, out_shape=[jax.ShapeDtypeStruct(shape, bf16)...  5.14 us
    pallas_call x1, Pallas kernels, per_device(): pl.pallas_call(own_sums, out_shape=jax.ShapeDtypeStruct(shape, f32), in_s...  3.56 us
    ppermute x1, starting transfers between devices, per_device(): arrived = lax.ppermute(theirs, 'c', [(0, 1), (1, 0)])  1.92 us
  transfers between devices with their start and end apart: 1, of which 0 were waited for; matrix products, arithmetic and copies ran while one was open for 0% of the time, Pallas kernels for 4%

profile of v8, /device:TPU:8, one launch (start us, length us, event | category | flops | bytes accessed | tf_op | source)
XLA Modules:
  0.0 93.9 jit_solution(14676081991589356695)
XLA Ops:
  0.6 5.1 %sibling_sums.1 = (bf16[2,4,688,128]{3,2,1,0:T(8,128)(2,1)S(1)}, bf16[512,1024]{1,0:T(8,128)(2,1)S(1)}, bf16[1024,1024]{1,0:T(8,128)(2,1)S(1)}, bf16[96,1024]{1,...) custom-call(s32[1]{0:T(128)} %bitcast.1.core_ref, s32[1]{0:T(128)} %bitcast.place_ref.refs_0_, ...), custom_call_target="tpu_custom_call" | custom-call | tf_op jit(solution)/shard_map/sibling_sums/pallas_call | solution.py:226
  5.8 1.9 %collective-permute-start = (bf16[2,4,688,128]{3,2,1,0:T(8,128)(2,1)S(1)}, bf16[2,4,688,128]{3,2,1,0:T(8,128)(2,1)S(1)}, u32[]{:S(2)}, u32[]{:S(2)}) collective-permute-start(bf16[2,4,688,128]{3,2,1,0:T(8,128)(2,1)S(1)} %get-tuple-element.18), channel_id=1, source_target_pairs={{0,1},{1,0},{2,3},{3,2},{4,5},{5,4},{6,7},{7,6},{8,9},{9,8},{10,11... | collective-permute-start | bytes 4227080 | tf_op jit(solution)/shard_map/ppermute | solution.py:236
  7.7 3.6 %own_sums.1.mine = f32[2,4,688,128]{3,2,1,0:T(8,128)S(1)} custom-call(s32[1]{0:T(128)} %bitcast.1.core_ref, bf16[512,1024]{1,0:T(8,128)(2,1)S(1)} %get-tuple-element.13.e, bf16[1024,1024]{1,0:T(8,128)(2,1)S(1)} %get-tuple-element.14.rot, bf16[96,1024]{1,0:T(8,128)(2,1)S(1)} %get-tuple-element.15.cent, s32[64,512]{1,0:T(8,128)S(1)} %get-tuple-element.16.codes, ...), custom_call_target="tpu_custom_call" | custom-call | flops 4000000000 | bytes 8000000 | tf_op jit(solution)/shard_map/own_sums/pallas_call | solution.py:237
  11.3 0.0 collective-permute-done.theirs
  11.3 0.3 chip_sums.1
  11.6 26.2 %all_to_all.20.arrived = bf16[8,688,128]{2,1,0:T(8,128)(2,1)S(1)} all-to-all(bf16[8,688,128]{2,1,0:T(8,128)(2,1)S(1)} %bitcast.4), channel_id=1, replica_groups=mesh['zs'=6,'zf'=2,'ys'=4,'yf'=2,'x'=4,'c'=2] {'zf','x'}, dimensions={0} | all-to-all | bytes 2818048 | tf_op jit(solution)/shard_map/all_to_all | solution.py:256
  37.8 0.2 first_sums.1
  38.0 17.3 %all_to_all.21.arrived = bf16[8,96,128]{2,1,0:T(8,128)(2,1)S(1)} all-to-all(bf16[8,96,128]{2,1,0:T(8,128)(2,1)S(1)} %first_sums.1), channel_id=1, replica_groups=mesh['zs'=6,'zf'=2,'ys'=4,'yf'=2,'x'=4,'c'=2] {'yf','ys'}, dimensions={0} | all-to-all | bytes 393216 | tf_op jit(solution)/shard_map/all_to_all | solution.py:265
  55.3 23.4 %all_to_all.22.refs_1_ = bf16[6,112,128]{2,1,0:T(8,128)(2,1)S(1)} all-to-all(bf16[6,112,128]{2,1,0:T(8,128)(2,1)S(1)} %second_sums.1), channel_id=1, replica_groups=mesh['zs'=6,'zf'=2,'ys'=4,'yf'=2,'x'=4,'c'=2] {'zs'}, dimensions={0} | all-to-all | bytes 344064 | tf_op jit(solution)/shard_map/all_to_all | solution.py:274
  78.7 0.5 owned_sums.1
  79.2 0.1 broadcast_in_dim.2
  79.3 13.7 %all_to_all.23 = f16[16,88,128]{2,1,0:T(8,128)(2,1)S(1)} all-to-all(f16[16,88,128]{2,1,0:T(8,128)(2,1)S(1)} %broadcast_in_dim.2), channel_id=1, replica_groups=mesh['zs'=6,'zf'=2,'ys'=4,'yf'=2,'x'=4,'c'=2] {'zf','yf','ys'}, dimensions={0} | all-to-all | bytes 720896 | tf_op jit(solution)/shard_map/all_to_all | solution.py:287
  93.0 0.9 laid_out.1
  (3 shorter events, 0.1 us)
Async XLA Ops:
  5.8 5.5 %collective-permute-start = (bf16[2,4,688,128]{3,2,1,0:T(8,128)(2,1)S(1)}, bf16[2,4,688,128]{3,2,1,0:T(8,128)(2,1)S(1)}, u32[]{:S(2)}, u32[]{:S(2)}) collective-permute-start(bf16[2,4,688,128]{3,2,1,0:T(8,128)(2,1)S(1)} %get-tuple-element.18), channel_id=1, source_target_pairs={{0,1},{1,0},{2,3},{3,2},{4,5},{5,4},{6,7},{7,6},{8,9},{9,8},{10,11... | collective-permute-start | bytes 4227080 | tf_op jit(solution)/shard_map/ppermute | solution.py:236
